TPU v7x, 32 devices: a whole 2x2x4 slice. The times are simulated.
32 devices in a mesh: dp: 8 (over y, x, core), pipe: 4 (over z).
Axes of the slice: x: 2, y: 2, z: 4, core: 2. Of those that a mesh axis runs over, the one named last changes fastest.
Arguments:
- layer_input: bfloat16 [64, 128, 768], P('dp'), may hold values from -6 to 6
- lengths: int32 [64], P('dp'), may hold values from 8 to 128
- regions: int32 [64, 128], P('dp'), may hold values 0 or 1
- cotangent: bfloat16 [64, 128, 768], P('dp'), may hold values from -6 to 6
- attend_weight: bfloat16 [4, 768, 2304], P('pipe'), may hold values from -0.3125 to 0.3125
- attend_bias: bfloat16 [4, 1536], P('pipe'), may hold values from -4 to 4
- output_weight: bfloat16 [4, 768, 768], P('pipe'), may hold values from -0.875 to 0.875
- output_bias: bfloat16 [4, 768], P('pipe'), may hold values from -3 to 3
- first_gain: bfloat16 [4, 768], P('pipe'), may hold values from 0.5 to 1.5
- first_shift: bfloat16 [4, 768], P('pipe'), may hold values from -3 to 3
- expand_weight: bfloat16 [4, 768, 3072], P('pipe'), may hold values from -0.21875 to 0.21875
- expand_bias: bfloat16 [4, 3072], P('pipe'), may hold values from -6 to 6
- reduce_weight: bfloat16 [4, 3072, 768], P('pipe'), may hold values from -0.109375 to 0.109375
- reduce_bias: bfloat16 [4, 768], P('pipe'), may hold values from -3 to 3
- second_gain: bfloat16 [4, 768], P('pipe'), may hold values from 0.5 to 1.5
- second_shift: bfloat16 [4, 768], P('pipe'), may hold values from -3 to 3
Outputs:
- layer_outputs: bfloat16 [4, 64, 128, 768], P('pipe', 'dp')
- input_grads: float32 [4, 64, 128, 768], P('pipe', 'dp')
- attend_weight_grad: float32 [4, 768, 2304], P('pipe')
- attend_bias_grad: float32 [4, 1536], P('pipe')
- output_weight_grad: float32 [4, 768, 768], P('pipe')
- output_bias_grad: float32 [4, 768], P('pipe')
- first_gain_grad: float32 [4, 768], P('pipe')
- first_shift_grad: float32 [4, 768], P('pipe')
- expand_weight_grad: float32 [4, 768, 3072], P('pipe')
- expand_bias_grad: float32 [4, 3072], P('pipe')
- reduce_weight_grad: float32 [4, 3072, 768], P('pipe')
- reduce_bias_grad: float32 [4, 768], P('pipe')
- second_gain_grad: float32 [4, 768], P('pipe')
- second_shift_grad: float32 [4, 768], P('pipe')
All inputs are finite; a program needn't handle non-finite values. No bound on the sum of `regions` on one device may be relied on, other than what follows from the above.
Results may differ from a plain program's by a relative error of at most 0.035.
Values may be sent and summed in bfloat16 or wider, within the bound.
A program may use at most 256 MiB of HBM per device.

v0:
```python
import jax
import jax.numpy as jnp
from jax import lax
from jax.sharding import PartitionSpec as P

HEADS = 12
MICRO = 4


epsilon = 1e-05
neg_large = -1000000000.0


def passed_along(value, axis, steps):
    count = lax.axis_size(axis)
    first, last = (max(0, -steps), min(count, count - steps))
    return lax.ppermute(value, axis, [(source, source + steps) for source in range(first, last)])


def times_t(left, right):
    return lax.dot_general(
        left, right, (((1,), (1,)), ((), ())), preferred_element_type=jnp.float32
    )


def outer_sum(left, right):
    return lax.dot_general(
        left, right, (((0,), (0,)), ((), ())), preferred_element_type=jnp.float32
    )


def layer_norm(entries, norm_gain, norm_shift):
    centre = entries - jnp.mean(entries, -1, keepdims=True)
    scale_inv = lax.rsqrt(jnp.mean(centre * centre, -1, keepdims=True) + epsilon)
    normed = centre * scale_inv
    return (normed * norm_gain + norm_shift, normed, scale_inv)


def norm_back(grad_norm, normed, scale_inv, norm_gain):
    scaled = grad_norm * norm_gain
    return scale_inv * (
        scaled
        - jnp.mean(scaled, -1, keepdims=True)
        - normed * jnp.mean(scaled * normed, -1, keepdims=True)
    )


def gelu_exact(entries):
    return jax.nn.gelu(entries, approximate=False)


def to_heads(entries, groups, slot_count):
    return entries.reshape(groups, slot_count, HEADS, entries.shape[1] // HEADS)


def section_forward(inputs, key_valid, params):
    (
        attend_weight,
        attend_bias,
        output_weight,
        output_bias,
        first_gain,
        first_shift,
        expand_weight,
        expand_bias,
        reduce_weight,
        reduce_bias,
        second_gain,
        second_shift,
    ) = params
    groups, slot_count, model_width = inputs.shape
    score_scale = (model_width // HEADS) ** (-0.5)
    token_rows = inputs.reshape(groups * slot_count, model_width)
    projected = jnp.dot(token_rows, attend_weight, preferred_element_type=jnp.float32)
    queries = (projected[:, :model_width] + attend_bias[:model_width]).astype(jnp.bfloat16)
    key_rows = projected[:, model_width : 2 * model_width].astype(jnp.bfloat16)
    values = (projected[:, 2 * model_width :] + attend_bias[model_width:]).astype(jnp.bfloat16)
    query_heads = to_heads(queries, groups, slot_count)
    key_heads = to_heads(key_rows, groups, slot_count)
    value_heads = to_heads(values, groups, slot_count)
    scores = (
        jnp.einsum("gqhe,gkhe->ghqk", query_heads, key_heads, preferred_element_type=jnp.float32)
        * score_scale
    )
    scores = jnp.where(key_valid[:, None, None, :], scores, neg_large)
    raised = jnp.exp(scores - jnp.max(scores, -1, keepdims=True))
    shares = raised / jnp.sum(raised, -1, keepdims=True)
    shares_low = shares.astype(jnp.bfloat16)
    context = jnp.einsum(
        "ghqk,gkhe->gqhe", shares_low, value_heads, preferred_element_type=jnp.float32
    )
    context_low = context.reshape(groups * slot_count, model_width).astype(jnp.bfloat16)
    attended = jnp.dot(context_low, output_weight, preferred_element_type=jnp.float32) + output_bias
    middle = token_rows.astype(jnp.float32) + attended
    first_out, first_norm, first_scale = layer_norm(middle, first_gain, first_shift)
    first_low = first_out.astype(jnp.bfloat16)
    expanded = jnp.dot(first_low, expand_weight, preferred_element_type=jnp.float32) + expand_bias
    active = gelu_exact(expanded).astype(jnp.bfloat16)
    reduced = jnp.dot(active, reduce_weight, preferred_element_type=jnp.float32) + reduce_bias
    result, second_norm, second_scale = layer_norm(first_out + reduced, second_gain, second_shift)
    kept_values = (
        token_rows,
        query_heads,
        key_heads,
        value_heads,
        shares,
        shares_low,
        context_low,
        first_norm,
        first_scale,
        first_low,
        expanded,
        active,
        second_norm,
        second_scale,
    )
    return (result.astype(jnp.bfloat16).reshape(inputs.shape), kept_values)


def section_backward(inputs, key_valid, params, grad_out):
    (
        attend_weight,
        attend_bias,
        output_weight,
        output_bias,
        first_gain,
        first_shift,
        expand_weight,
        expand_bias,
        reduce_weight,
        reduce_bias,
        second_gain,
        second_shift,
    ) = params
    groups, slot_count, model_width = inputs.shape
    score_scale = (model_width // HEADS) ** (-0.5)
    kept_values = section_forward(inputs, key_valid, params)[1]
    (
        token_rows,
        query_heads,
        key_heads,
        value_heads,
        shares,
        shares_low,
        context_low,
        first_norm,
        first_scale,
        first_low,
        expanded,
        active,
        second_norm,
        second_scale,
    ) = kept_values
    grad_mix = norm_back(grad_out, second_norm, second_scale, second_gain)
    grad_reduced = grad_mix.astype(jnp.bfloat16)
    grad_active = times_t(grad_reduced, reduce_weight)
    gelu_pull = jax.vjp(gelu_exact, expanded)[1]
    grad_expanded = gelu_pull(grad_active)[0].astype(jnp.bfloat16)
    grad_first = grad_mix + times_t(grad_expanded, expand_weight)
    grad_middle = norm_back(grad_first, first_norm, first_scale, first_gain)
    grad_attended = grad_middle.astype(jnp.bfloat16)
    grad_context = times_t(grad_attended, output_weight).astype(jnp.bfloat16)
    grad_context = to_heads(grad_context, groups, slot_count)
    grad_shares = jnp.einsum(
        "gqhe,gkhe->ghqk", grad_context, value_heads, preferred_element_type=jnp.float32
    )
    grad_values = jnp.einsum(
        "ghqk,gqhe->gkhe", shares_low, grad_context, preferred_element_type=jnp.float32
    )
    grad_scores = (
        shares * (grad_shares - jnp.sum(grad_shares * shares, -1, keepdims=True))
    ).astype(jnp.bfloat16)
    grad_queries = (
        jnp.einsum("ghqk,gkhe->gqhe", grad_scores, key_heads, preferred_element_type=jnp.float32)
        * score_scale
    )
    grad_keys = (
        jnp.einsum("ghqk,gqhe->gkhe", grad_scores, query_heads, preferred_element_type=jnp.float32)
        * score_scale
    )
    row_count = groups * slot_count
    grad_project = jnp.concatenate(
        [
            grad_queries.reshape(row_count, model_width),
            grad_keys.reshape(row_count, model_width),
            grad_values.reshape(row_count, model_width),
        ],
        1,
    ).astype(jnp.bfloat16)
    grad_inputs = grad_middle + times_t(grad_project, attend_weight)
    parts = (
        token_rows,
        grad_project,
        context_low,
        grad_attended,
        first_norm,
        grad_first,
        first_low,
        grad_expanded,
        active,
        grad_reduced,
        second_norm,
        grad_out,
    )
    return (grad_inputs, parts)


def attention_grads(token_rows, grad_project, context_low, grad_attended, first_norm, grad_first):
    model_width = token_rows.shape[1]
    bias_terms = jnp.sum(grad_project.astype(jnp.float32), 0)
    return (
        outer_sum(token_rows, grad_project),
        jnp.concatenate([bias_terms[:model_width], bias_terms[2 * model_width :]]),
        outer_sum(context_low, grad_attended),
        jnp.sum(grad_attended.astype(jnp.float32), 0),
        jnp.sum(grad_first * first_norm, 0),
        jnp.sum(grad_first, 0),
    )


def ffn_grads(first_low, grad_expanded, active, grad_reduced, second_norm, grad_out):
    return (
        outer_sum(first_low, grad_expanded),
        jnp.sum(grad_expanded.astype(jnp.float32), 0),
        outer_sum(active, grad_reduced),
        jnp.sum(grad_reduced.astype(jnp.float32), 0),
        jnp.sum(grad_out * second_norm, 0),
        jnp.sum(grad_out, 0),
    )


def local(
    layer_input,
    lengths,
    regions,
    cotangent,
    attend_weight,
    attend_bias,
    output_weight,
    output_bias,
    first_gain,
    first_shift,
    expand_weight,
    expand_bias,
    reduce_weight,
    reduce_bias,
    second_gain,
    second_shift,
):
    params = tuple(
        (
            weight[0]
            for weight in (
                attend_weight,
                attend_bias,
                output_weight,
                output_bias,
                first_gain,
                first_shift,
                expand_weight,
                expand_bias,
                reduce_weight,
                reduce_bias,
                second_gain,
                second_shift,
            )
        )
    )
    section_here = lax.axis_index("pipe")
    section_count = lax.axis_size("pipe")
    last_section = section_count - 1
    tick_count = MICRO + section_count - 1
    seq_here, slot_count, model_width = layer_input.shape
    hidden_width = params[6].shape[1]
    groups = seq_here // MICRO
    row_count = groups * slot_count
    positions = jnp.arange(slot_count, dtype=jnp.int32)
    key_valid = ((positions[None, :] < lengths[:, None]) | (regions == 1)).reshape(
        MICRO, groups, slot_count
    )
    micro_inputs = layer_input.reshape(MICRO, groups, slot_count, model_width)
    micro_tangents = cotangent.reshape(MICRO, groups, slot_count, model_width)
    empty_act = jnp.zeros((groups, slot_count, model_width), jnp.bfloat16)
    empty_grad = jnp.zeros((groups, slot_count, model_width), jnp.float32)

    def forward_tick(moment, carry):
        arrived, saved_in, saved_out = carry
        batch_index = moment - section_here
        running = (batch_index >= 0) & (batch_index < MICRO)
        picked = jnp.clip(batch_index, 0, MICRO - 1)
        fresh_batch = lax.dynamic_index_in_dim(micro_inputs, picked, 0, keepdims=False)
        section_feed = jnp.where(section_here == 0, fresh_batch, arrived)
        mask_here = lax.dynamic_index_in_dim(key_valid, picked, 0, keepdims=False)

        def forward_advance(buffers):
            result = section_forward(section_feed, mask_here, params)[0]
            return (
                (
                    lax.dynamic_update_index_in_dim(buffers[0], section_feed, picked, 0),
                    lax.dynamic_update_index_in_dim(buffers[1], result, picked, 0),
                ),
                result,
            )

        def forward_standby(buffers):
            return (buffers, empty_act)

        buffers, result = lax.cond(running, forward_advance, forward_standby, (saved_in, saved_out))
        handed = passed_along(result, "pipe", 1)
        return (handed, buffers[0], buffers[1])

    saved_start = jnp.zeros((MICRO, groups, slot_count, model_width), jnp.bfloat16)
    arrived, saved_in, saved_out = lax.fori_loop(
        0, tick_count, forward_tick, (empty_act, saved_start, saved_start)
    )
    part_shapes = (
        (row_count, 3 * model_width, jnp.bfloat16),
        (row_count, model_width, jnp.bfloat16),
        (row_count, model_width, jnp.bfloat16),
        (row_count, model_width, jnp.float32),
        (row_count, model_width, jnp.float32),
        (row_count, model_width, jnp.bfloat16),
        (row_count, hidden_width, jnp.bfloat16),
        (row_count, hidden_width, jnp.bfloat16),
        (row_count, model_width, jnp.bfloat16),
        (row_count, model_width, jnp.float32),
        (row_count, model_width, jnp.float32),
    )
    stored_parts = tuple(
        (
            jnp.zeros((MICRO, rows_here, cols_here), kind_here)
            for rows_here, cols_here, kind_here in part_shapes
        )
    )

    def absorb(stored, parts, picked):
        return tuple(
            (
                lax.dynamic_update_index_in_dim(buffer, piece, picked, 0)
                for buffer, piece in zip(stored, parts[1:])
            )
        )

    def backward_tick(moment, carry):
        arrived, grads_in, stored = carry
        batch_index = moment - (last_section - section_here)
        running = (batch_index >= 0) & (batch_index < MICRO)
        picked = jnp.clip(batch_index, 0, MICRO - 1)
        tangent_in = lax.dynamic_index_in_dim(micro_tangents, picked, 0, keepdims=False)
        grad_out = jnp.where(section_here == last_section, tangent_in, arrived).astype(jnp.float32)
        mask_here = lax.dynamic_index_in_dim(key_valid, picked, 0, keepdims=False)

        def backward_advance(loop_state):
            inputs = lax.dynamic_index_in_dim(saved_in, picked, 0, keepdims=False)
            grad_inputs, parts = section_backward(
                inputs, mask_here, params, grad_out.reshape(row_count, model_width)
            )
            grad_inputs = grad_inputs.reshape(groups, slot_count, model_width)
            grads_new = lax.dynamic_update_index_in_dim(loop_state[0], grad_inputs, picked, 0)
            return ((grads_new, absorb(loop_state[1], parts, picked)), grad_inputs)

        def backward_standby(loop_state):
            return (loop_state, empty_grad)

        (grads_in, stored), grad_inputs = lax.cond(
            running, backward_advance, backward_standby, (grads_in, stored)
        )
        handed = passed_along(grad_inputs.astype(jnp.bfloat16), "pipe", -1)
        return (handed, grads_in, stored)

    grads_start = jnp.zeros((MICRO, groups, slot_count, model_width), jnp.float32)
    arrived, grads_in, stored_parts = lax.fori_loop(
        0, tick_count, backward_tick, (empty_act, grads_start, stored_parts)
    )
    flat_parts = tuple(
        (buffer.reshape((MICRO * row_count, buffer.shape[2])) for buffer in stored_parts)
    )
    expand_w, expand_b, reduce_w, reduce_b, second_g, second_s = ffn_grads(*flat_parts[5:])
    ffn_totals = (
        lax.psum(expand_w.astype(jnp.bfloat16), "dp").astype(jnp.float32),
        lax.psum(expand_b.astype(jnp.bfloat16), "dp").astype(jnp.float32),
        lax.psum(reduce_w.astype(jnp.bfloat16), "dp").astype(jnp.float32),
        lax.psum(reduce_b.astype(jnp.bfloat16), "dp").astype(jnp.float32),
        lax.psum(second_g.astype(jnp.bfloat16), "dp").astype(jnp.float32),
        lax.psum(second_s.astype(jnp.bfloat16), "dp").astype(jnp.float32),
    )
    all_rows = saved_in.reshape(MICRO * row_count, model_width)
    attend_w, attend_b, output_w, output_b, first_g, first_s = attention_grads(
        all_rows, *flat_parts[:5]
    )
    attention_totals = (
        lax.psum(attend_w.astype(jnp.bfloat16), "dp").astype(jnp.float32),
        lax.psum(attend_b.astype(jnp.bfloat16), "dp").astype(jnp.float32),
        lax.psum(output_w.astype(jnp.bfloat16), "dp").astype(jnp.float32),
        lax.psum(output_b.astype(jnp.bfloat16), "dp").astype(jnp.float32),
        lax.psum(first_g.astype(jnp.bfloat16), "dp").astype(jnp.float32),
        lax.psum(first_s.astype(jnp.bfloat16), "dp").astype(jnp.float32),
    )
    totals = tuple(attention_totals) + tuple(ffn_totals)
    outputs = tuple((total[None] for total in totals))
    return (
        saved_out.reshape((1, seq_here, slot_count, model_width)),
        grads_in.reshape((1, seq_here, slot_count, model_width)),
    ) + outputs


def solution(mesh):
    placed = (
        P("dp", None, None),
        P("dp"),
        P("dp", None),
        P("dp", None, None),
        P("pipe", None, None),
        P("pipe", None),
        P("pipe", None, None),
        P("pipe", None),
        P("pipe", None),
        P("pipe", None),
        P("pipe", None, None),
        P("pipe", None),
        P("pipe", None, None),
        P("pipe", None),
        P("pipe", None),
        P("pipe", None),
    )
    return jax.shard_map(
        local,
        mesh=mesh,
        in_specs=placed,
        out_specs=(
            P("pipe", "dp", None, None),
            P("pipe", "dp", None, None),
            P("pipe", None, None),
            P("pipe", None),
            P("pipe", None, None),
            P("pipe", None),
            P("pipe", None),
            P("pipe", None),
            P("pipe", None, None),
            P("pipe", None),
            P("pipe", None, None),
            P("pipe", None),
            P("pipe", None),
            P("pipe", None),
        ),
        check_vma=False,
    )
```

profile of v0, /device:TPU:1, one launch (start us, length us, event | category | flops | bytes accessed | tf_op | source)
XLA Modules:
  0.0 1178.2 jit_solution(11863965863856513614)
XLA Ops:
  20.3 274.4 %while.57 = (s32[]{:T(128)}, bf16[2,128,768]{2,1,0:T(8,128)(2,1)S(1)}, bf16[4,2,128,768]{3,2,1,0:T(8,128)(2,1)}, bf16[4,2,128,768]{3,2,1,0:T(8,128)(2,1)}, s32[]...) while((s32[]{:T(128)}, ...), condition=%wide.region_9.10_spmd, body=%wide.region_0.9_spmd.sunk | while | flops 3785303552 | bytes 44994440 | solution.py:313
  20.3 33.8 %conditional.4 = (bf16[4,2,128,768]{3,2,1,0:T(8,128)(2,1)}, bf16[4,2,128,768]{3,2,1,0:T(8,128)(2,1)}, bf16[2,128,768]{2,1,0:T(8,128)(2,1)}) conditional(s32[]{:T(128)} %convert_element_type.412, (bf16[4,2,128,768]{3,2,1,0:T(8,128)(2,1)}, bf16[4,2,128,768]{3,2,1,0:T(8,128)(2,1)}) %tuple.129, (pred[]{:T(512)}, s32[]{:T(128)}, ...), branch_computations={%region_1.1_spmd, %region_2.8_spmd} | conditional | flops 3785303552 | bytes 43421128 | solution.py:308
  38.1 13.0 %fusion.154 = (f32[256]{0:T(256)S(1)}, f32[256,768]{1,0:T(8,128)S(1)}) fusion(f32[768]{0:T(1024)} %convert_element_type.289, bf16[3072,768]{1,0:T(8,128)(2,1)} %get-tuple-element.1409, f32[3072]{0:T(1024)} %convert_element_type.287, bf16[768,3072]{1,0:T(8,128)(2,1)} %get-tuple-element.1407, f32[256,768]{1,0:T(8,128)S(1)} %get-tuple-element.1754, ...), kind=kOutput, calls=%fused_computation.226 | convolution fusion | flops 2470182656 | bytes 11034624 | tf_op jit(solution)/shard_map/while/body/eval_jaxpr/cond/branch_1_fun/dot_general | solution.py:99
  55.4 9.0 collective-permute-done
  64.4 33.8 %conditional.4 = (bf16[4,2,128,768]{3,2,1,0:T(8,128)(2,1)}, bf16[4,2,128,768]{3,2,1,0:T(8,128)(2,1)}, bf16[2,128,768]{2,1,0:T(8,128)(2,1)}) conditional(s32[]{:T(128)} %convert_element_type.412, (bf16[4,2,128,768]{3,2,1,0:T(8,128)(2,1)}, bf16[4,2,128,768]{3,2,1,0:T(8,128)(2,1)}) %tuple.129, (pred[]{:T(512)}, s32[]{:T(128)}, ...), branch_computations={%region_1.1_spmd, %region_2.8_spmd} | conditional | flops 3785303552 | bytes 43421128 | solution.py:308
  82.2 13.0 %fusion.154 = (f32[256]{0:T(256)S(1)}, f32[256,768]{1,0:T(8,128)S(1)}) fusion(f32[768]{0:T(1024)} %convert_element_type.289, bf16[3072,768]{1,0:T(8,128)(2,1)} %get-tuple-element.1409, f32[3072]{0:T(1024)} %convert_element_type.287, bf16[768,3072]{1,0:T(8,128)(2,1)} %get-tuple-element.1407, f32[256,768]{1,0:T(8,128)S(1)} %get-tuple-element.1754, ...), kind=kOutput, calls=%fused_computation.226 | convolution fusion | flops 2470182656 | bytes 11034624 | tf_op jit(solution)/shard_map/while/body/eval_jaxpr/cond/branch_1_fun/dot_general | solution.py:99
  102.2 8.1 collective-permute-done
  110.3 33.8 %conditional.4 = (bf16[4,2,128,768]{3,2,1,0:T(8,128)(2,1)}, bf16[4,2,128,768]{3,2,1,0:T(8,128)(2,1)}, bf16[2,128,768]{2,1,0:T(8,128)(2,1)}) conditional(s32[]{:T(128)} %convert_element_type.412, (bf16[4,2,128,768]{3,2,1,0:T(8,128)(2,1)}, bf16[4,2,128,768]{3,2,1,0:T(8,128)(2,1)}) %tuple.129, (pred[]{:T(512)}, s32[]{:T(128)}, ...), branch_computations={%region_1.1_spmd, %region_2.8_spmd} | conditional | flops 3785303552 | bytes 43421128 | solution.py:308
  128.1 13.0 %fusion.154 = (f32[256]{0:T(256)S(1)}, f32[256,768]{1,0:T(8,128)S(1)}) fusion(f32[768]{0:T(1024)} %convert_element_type.289, bf16[3072,768]{1,0:T(8,128)(2,1)} %get-tuple-element.1409, f32[3072]{0:T(1024)} %convert_element_type.287, bf16[768,3072]{1,0:T(8,128)(2,1)} %get-tuple-element.1407, f32[256,768]{1,0:T(8,128)S(1)} %get-tuple-element.1754, ...), kind=kOutput, calls=%fused_computation.226 | convolution fusion | flops 2470182656 | bytes 11034624 | tf_op jit(solution)/shard_map/while/body/eval_jaxpr/cond/branch_1_fun/dot_general | solution.py:99
  148.1 7.2 collective-permute-done
  155.3 33.8 %conditional.4 = (bf16[4,2,128,768]{3,2,1,0:T(8,128)(2,1)}, bf16[4,2,128,768]{3,2,1,0:T(8,128)(2,1)}, bf16[2,128,768]{2,1,0:T(8,128)(2,1)}) conditional(s32[]{:T(128)} %convert_element_type.412, (bf16[4,2,128,768]{3,2,1,0:T(8,128)(2,1)}, bf16[4,2,128,768]{3,2,1,0:T(8,128)(2,1)}) %tuple.129, (pred[]{:T(512)}, s32[]{:T(128)}, ...), branch_computations={%region_1.1_spmd, %region_2.8_spmd} | conditional | flops 3785303552 | bytes 43421128 | solution.py:308
  173.1 13.0 %fusion.154 = (f32[256]{0:T(256)S(1)}, f32[256,768]{1,0:T(8,128)S(1)}) fusion(f32[768]{0:T(1024)} %convert_element_type.289, bf16[3072,768]{1,0:T(8,128)(2,1)} %get-tuple-element.1409, f32[3072]{0:T(1024)} %convert_element_type.287, bf16[768,3072]{1,0:T(8,128)(2,1)} %get-tuple-element.1407, f32[256,768]{1,0:T(8,128)S(1)} %get-tuple-element.1754, ...), kind=kOutput, calls=%fused_computation.226 | convolution fusion | flops 2470182656 | bytes 11034624 | tf_op jit(solution)/shard_map/while/body/eval_jaxpr/cond/branch_1_fun/dot_general | solution.py:99
  193.1 6.3 collective-permute-done
  200.1 37.0 %collective-permute-start = (bf16[2,128,768]{2,1,0:T(8,128)(2,1)}, bf16[2,128,768]{2,1,0:T(8,128)(2,1)S(1)}, u32[]{:S(2)}, u32[]{:S(2)}) collective-permute-start(bf16[2,128,768]{2,1,0:T(8,128)(2,1)} %get-tuple-element.2074), channel_id=1, source_target_pairs={{0,1},{1,2},{2,3},{4,5},{5,6},{6,7},{8,9},{9,10},{10,11},{12,13},{... | collective-permute-start | bytes 1179656 | tf_op jit(solution)/shard_map/while/body/eval_jaxpr/ppermute | solution.py:17
  237.2 5.3 collective-permute-done
  247.3 5.0 collective-permute-done
  253.1 36.3 %collective-permute-start = (bf16[2,128,768]{2,1,0:T(8,128)(2,1)}, bf16[2,128,768]{2,1,0:T(8,128)(2,1)S(1)}, u32[]{:S(2)}, u32[]{:S(2)}) collective-permute-start(bf16[2,128,768]{2,1,0:T(8,128)(2,1)} %get-tuple-element.2074), channel_id=1, source_target_pairs={{0,1},{1,2},{2,3},{4,5},{5,6},{6,7},{8,9},{9,10},{10,11},{12,13},{... | collective-permute-start | bytes 1179656 | tf_op jit(solution)/shard_map/while/body/eval_jaxpr/ppermute | solution.py:17
  289.4 5.0 collective-permute-done
  319.0 599.3 %while.58 = (s32[]{:T(128)}, bf16[2,128,768]{2,1,0:T(8,128)(2,1)S(1)}, f32[4,2,128,768]{3,2,1,0:T(8,128)}, bf16[4,256,2304]{1,2,0:T(8,128)(2,1)}, bf16[4,256,768...) while((s32[]{:T(128)}, ...), condition=%wide.region_24.25_spmd, body=%wide.region_10.24_spmd.sunk | while | flops 7640586240 | bytes 195768160 | solution.py:372
  337.6 7.6 collective-permute-done.1
  349.7 40.0 %collective-permute-done.1 = bf16[2,128,768]{2,1,0:T(8,128)(2,1)S(1)} collective-permute-done((bf16[2,128,768]{2,1,0:T(8,128)(2,1)S(1)}, bf16[2,128,768]{2,1,0:T(8,128)(2,1)S(1)}, u32[]{:S(2)}, u32[]{:S(2)}) %collective-permute-start.1) | collective-permute-done | bytes 393248 | tf_op jit(solution)/shard_map/while/body/eval_jaxpr/ppermute | solution.py:17
  394.2 208.1 %collective-permute-done.1 = bf16[2,128,768]{2,1,0:T(8,128)(2,1)S(1)} collective-permute-done((bf16[2,128,768]{2,1,0:T(8,128)(2,1)S(1)}, bf16[2,128,768]{2,1,0:T(8,128)(2,1)S(1)}, u32[]{:S(2)}, u32[]{:S(2)}) %collective-permute-start.1) | collective-permute-done | bytes 393248 | tf_op jit(solution)/shard_map/while/body/eval_jaxpr/ppermute | solution.py:17
  603.4 68.0 %conditional.5 = (f32[4,2,128,768]{3,2,1,0:T(8,128)}, bf16[4,256,2304]{1,2,0:T(8,128)(2,1)}, bf16[4,256,768]{1,2,0:T(8,128)(2,1)}, bf16[4,256,768]{2,1,0:T(8,128...) conditional(s32[]{:T(128)} %convert_element_type.414, ...), branch_computations={%region_11.11_spmd, %region_12.23_spmd} | conditional | flops 7639996416 | bytes 191442080 | solution.py:365
  624.2 10.6 bitcast_dynamic-update-slice_fusion.1
  654.0 4.1 convolution_add_fusion.4
  673.9 7.4 collective-permute-done.1
  682.3 68.1 %conditional.5 = (f32[4,2,128,768]{3,2,1,0:T(8,128)}, bf16[4,256,2304]{1,2,0:T(8,128)(2,1)}, bf16[4,256,768]{1,2,0:T(8,128)(2,1)}, bf16[4,256,768]{2,1,0:T(8,128...) conditional(s32[]{:T(128)} %convert_element_type.414, ...), branch_computations={%region_11.11_spmd, %region_12.23_spmd} | conditional | flops 7639996416 | bytes 191442080 | solution.py:365
  703.1 10.6 bitcast_dynamic-update-slice_fusion.1
  752.9 7.3 collective-permute-done.1
  761.3 68.1 %conditional.5 = (f32[4,2,128,768]{3,2,1,0:T(8,128)}, bf16[4,256,2304]{1,2,0:T(8,128)(2,1)}, bf16[4,256,768]{1,2,0:T(8,128)(2,1)}, bf16[4,256,768]{2,1,0:T(8,128...) conditional(s32[]{:T(128)} %convert_element_type.414, ...), branch_computations={%region_11.11_spmd, %region_12.23_spmd} | conditional | flops 7639996416 | bytes 191442080 | solution.py:365
  782.1 10.6 bitcast_dynamic-update-slice_fusion.1
  812.0 4.1 convolution_add_fusion.4
  831.9 7.2 collective-permute-done.1
  840.2 68.1 %conditional.5 = (f32[4,2,128,768]{3,2,1,0:T(8,128)}, bf16[4,256,2304]{1,2,0:T(8,128)(2,1)}, bf16[4,256,768]{1,2,0:T(8,128)(2,1)}, bf16[4,256,768]{2,1,0:T(8,128...) conditional(s32[]{:T(128)} %convert_element_type.414, ...), branch_computations={%region_11.11_spmd, %region_12.23_spmd} | conditional | flops 7639996416 | bytes 191442080 | solution.py:365
  861.0 10.6 bitcast_dynamic-update-slice_fusion.1
  890.8 4.1 convolution_add_fusion.4
  910.7 7.2 collective-permute-done.1
  918.4 7.0 copy.121
  925.3 8.6 fusion.140
  933.9 4.4 fusion.143
  938.4 8.4 fusion.141
  946.8 8.5 fusion.142
  960.2 4.7 fusion.145
  970.7 36.3 %all-reduce = (bf16[1,1536]{1,0:T(2,128)(2,1)S(1)}, bf16[1,768]{1,0:T(2,128)(2,1)S(1)}, bf16[1,768]{1,0:T(2,128)(2,1)S(1)}, bf16[1,768]{1,0:T(2,128)(2,1)S(1)}, ...) all-reduce(bf16[1,1536]{1,0:T(2,128)(2,1)S(1)} %broadcast_in_dim.23, ...), channel_id=1, replica_groups=mesh['dp'=8,'pipe'=4] {'dp'}, use_global_device_ids=true, to_apply=%region_27.28 | all-reduce | flops 9216 | bytes 36864 | tf_op jit(solution)/shard_map/psum | solution.py:393
  1011.7 142.7 %all-reduce.4.cloned.1.call-done = (bf16[1,768,2304]{2,1,0:T(8,128)(2,1)}, bf16[1,768,768]{2,1,0:T(8,128)(2,1)}, bf16[1,768,3072]{2,1,0:T(8,128)(2,1)}, bf16[1,3072,768]{2,1,0:T(8,128)(2,1)}) async-done(((bf16[1,768,2304]{2,1,0:T(8,128)(2,1)}, bf16[1,768,768]{2,1,0:T(8,128)(2,1)}, bf16[1,768,3072]{2,1,0:T(8,128)(2,1)}, bf16[1,3072,768]{2,1,0:T(8,128)(2,1)}), (bf16[1,768,2304]{2,1,0:T(8,128)(2,1)}, ...) | async-done | bytes 14155792 | tf_op jit(solution)/shard_map/psum | solution.py:392
  1154.4 5.6 broadcast_in_dim.234
  1161.6 5.0 broadcast_in_dim.246
  1166.7 4.5 broadcast_in_dim.250
  (738 shorter events, 405.0 us)
Async XLA Ops:
  7.2 1147.2 %all-reduce.4.cloned.1.call-start = ((), (), s32[]{:S(2)}) async-start(), calls=%async_computation | async-start | bytes 28311552 | tf_op jit(solution)/shard_map/psum | solution.py:392
  38.1 13.0 %copy-start.28 = (bf16[768]{0:T(1024)(128)(2,1)S(1)}, bf16[768]{0:T(1024)(128)(2,1)}, u32[]{:S(2)}) copy-start(bf16[768]{0:T(1024)(128)(2,1)} %get-tuple-element.1412) | copy-start | bytes 4612 | tf_op jit(solution)/shard_map/while/body/eval_jaxpr/cond
  38.1 13.0 %copy-start.23 = (bf16[768]{0:T(1024)(128)(2,1)S(1)}, bf16[768]{0:T(1024)(128)(2,1)}, u32[]{:S(2)}) copy-start(bf16[768]{0:T(1024)(128)(2,1)} %get-tuple-element.1411) | copy-start | bytes 4612 | tf_op jit(solution)/shard_map/while/body/eval_jaxpr/cond
  54.1 10.3 collective-permute-start
  82.2 13.0 %copy-start.28 = (bf16[768]{0:T(1024)(128)(2,1)S(1)}, bf16[768]{0:T(1024)(128)(2,1)}, u32[]{:S(2)}) copy-start(bf16[768]{0:T(1024)(128)(2,1)} %get-tuple-element.1412) | copy-start | bytes 4612 | tf_op jit(solution)/shard_map/while/body/eval_jaxpr/cond
  82.2 13.0 %copy-start.23 = (bf16[768]{0:T(1024)(128)(2,1)S(1)}, bf16[768]{0:T(1024)(128)(2,1)}, u32[]{:S(2)}) copy-start(bf16[768]{0:T(1024)(128)(2,1)} %get-tuple-element.1411) | copy-start | bytes 4612 | tf_op jit(solution)/shard_map/while/body/eval_jaxpr/cond
  98.2 12.1 %collective-permute-start = (bf16[2,128,768]{2,1,0:T(8,128)(2,1)}, bf16[2,128,768]{2,1,0:T(8,128)(2,1)S(1)}, u32[]{:S(2)}, u32[]{:S(2)}) collective-permute-start(bf16[2,128,768]{2,1,0:T(8,128)(2,1)} %get-tuple-element.2074), channel_id=1, source_target_pairs={{0,1},{1,2},{2,3},{4,5},{5,6},{6,7},{8,9},{9,10},{10,11},{12,13},{... | collective-permute-start | bytes 1179656 | tf_op jit(solution)/shard_map/while/body/eval_jaxpr/ppermute | solution.py:17
  128.1 13.0 %copy-start.28 = (bf16[768]{0:T(1024)(128)(2,1)S(1)}, bf16[768]{0:T(1024)(128)(2,1)}, u32[]{:S(2)}) copy-start(bf16[768]{0:T(1024)(128)(2,1)} %get-tuple-element.1412) | copy-start | bytes 4612 | tf_op jit(solution)/shard_map/while/body/eval_jaxpr/cond
  128.1 13.0 %copy-start.23 = (bf16[768]{0:T(1024)(128)(2,1)S(1)}, bf16[768]{0:T(1024)(128)(2,1)}, u32[]{:S(2)}) copy-start(bf16[768]{0:T(1024)(128)(2,1)} %get-tuple-element.1411) | copy-start | bytes 4612 | tf_op jit(solution)/shard_map/while/body/eval_jaxpr/cond
  144.1 11.2 collective-permute-start
  173.1 13.0 %copy-start.28 = (bf16[768]{0:T(1024)(128)(2,1)S(1)}, bf16[768]{0:T(1024)(128)(2,1)}, u32[]{:S(2)}) copy-start(bf16[768]{0:T(1024)(128)(2,1)} %get-tuple-element.1412) | copy-start | bytes 4612 | tf_op jit(solution)/shard_map/while/body/eval_jaxpr/cond
  173.1 13.0 %copy-start.23 = (bf16[768]{0:T(1024)(128)(2,1)S(1)}, bf16[768]{0:T(1024)(128)(2,1)}, u32[]{:S(2)}) copy-start(bf16[768]{0:T(1024)(128)(2,1)} %get-tuple-element.1411) | copy-start | bytes 4612 | tf_op jit(solution)/shard_map/while/body/eval_jaxpr/cond
  189.1 10.3 collective-permute-start
  200.1 42.4 %collective-permute-start = (bf16[2,128,768]{2,1,0:T(8,128)(2,1)}, bf16[2,128,768]{2,1,0:T(8,128)(2,1)S(1)}, u32[]{:S(2)}, u32[]{:S(2)}) collective-permute-start(bf16[2,128,768]{2,1,0:T(8,128)(2,1)} %get-tuple-element.2074), channel_id=1, source_target_pairs={{0,1},{1,2},{2,3},{4,5},{5,6},{6,7},{8,9},{9,10},{10,11},{12,13},{... | collective-permute-start | bytes 1179656 | tf_op jit(solution)/shard_map/while/body/eval_jaxpr/ppermute | solution.py:17
  243.3 9.0 collective-permute-start
  253.1 41.3 %collective-permute-start = (bf16[2,128,768]{2,1,0:T(8,128)(2,1)}, bf16[2,128,768]{2,1,0:T(8,128)(2,1)S(1)}, u32[]{:S(2)}, u32[]{:S(2)}) collective-permute-start(bf16[2,128,768]{2,1,0:T(8,128)(2,1)} %get-tuple-element.2074), channel_id=1, source_target_pairs={{0,1},{1,2},{2,3},{4,5},{5,6},{6,7},{8,9},{9,10},{10,11},{12,13},{... | collective-permute-start | bytes 1179656 | tf_op jit(solution)/shard_map/while/body/eval_jaxpr/ppermute | solution.py:17
  336.3 8.9 collective-permute-start.1
  348.4 41.3 %collective-permute-start.1 = (bf16[2,128,768]{2,1,0:T(8,128)(2,1)S(1)}, bf16[2,128,768]{2,1,0:T(8,128)(2,1)S(1)}, u32[]{:S(2)}, u32[]{:S(2)}) collective-permute-start(bf16[2,128,768]{2,1,0:T(8,128)(2,1)S(1)} %convert_element_type.415), channel_id=1, source_target_pairs={{1,0},{2,1},{3,2},{5,4},{6,5},{7,6},{9,8},{10,9},{11,10},{13,12},{... | collective-permute-start | bytes 1179656 | tf_op jit(solution)/shard_map/while/body/eval_jaxpr/ppermute | solution.py:17
  392.9 209.4 %collective-permute-start.1 = (bf16[2,128,768]{2,1,0:T(8,128)(2,1)S(1)}, bf16[2,128,768]{2,1,0:T(8,128)(2,1)S(1)}, u32[]{:S(2)}, u32[]{:S(2)}) collective-permute-start(bf16[2,128,768]{2,1,0:T(8,128)(2,1)S(1)} %convert_element_type.415), channel_id=1, source_target_pairs={{1,0},{2,1},{3,2},{5,4},{6,5},{7,6},{9,8},{10,9},{11,10},{13,12},{... | collective-permute-start | bytes 1179656 | tf_op jit(solution)/shard_map/while/body/eval_jaxpr/ppermute | solution.py:17
  622.2 12.6 %slice-start.10 = ((s8[4718592]{0:T(1024)(128)(4,1)}), s8[4194304]{0:T(1024)(128)(4,1)S(1)}, s32[]{:S(2)}) async-start(s8[4718592]{0:T(1024)(128)(4,1)} %bitcast.202), calls=%async_computation.11 | async-start | bytes 8388608 | tf_op jit(solution)/shard_map/while/body/eval_jaxpr/cond
  622.8 20.1 %copy-start.18 = (f32[256]{0:T(256)}, f32[256]{0:T(256)S(1)}, u32[]{:S(2)}) copy-start(f32[256]{0:T(256)S(1)} %broadcast_multiply_fusion.6) | copy-start | bytes 3076 | tf_op jit(solution)/shard_map/while/body/eval_jaxpr/cond
  623.1 19.9 %copy-start.25 = (f32[256]{0:T(256)}, f32[256]{0:T(256)S(1)}, u32[]{:S(2)}) copy-start(f32[256]{0:T(256)S(1)} %add_rsqrt_fusion.3) | copy-start | bytes 3076 | tf_op jit(solution)/shard_map/while/body/eval_jaxpr/cond
  624.2 10.7 slice-start.11
  672.6 8.7 collective-permute-start.1
  701.2 12.6 %slice-start.10 = ((s8[4718592]{0:T(1024)(128)(4,1)}), s8[4194304]{0:T(1024)(128)(4,1)S(1)}, s32[]{:S(2)}) async-start(s8[4718592]{0:T(1024)(128)(4,1)} %bitcast.202), calls=%async_computation.11 | async-start | bytes 8388608 | tf_op jit(solution)/shard_map/while/body/eval_jaxpr/cond
  701.8 20.1 %copy-start.18 = (f32[256]{0:T(256)}, f32[256]{0:T(256)S(1)}, u32[]{:S(2)}) copy-start(f32[256]{0:T(256)S(1)} %broadcast_multiply_fusion.6) | copy-start | bytes 3076 | tf_op jit(solution)/shard_map/while/body/eval_jaxpr/cond
  702.0 19.9 %copy-start.25 = (f32[256]{0:T(256)}, f32[256]{0:T(256)S(1)}, u32[]{:S(2)}) copy-start(f32[256]{0:T(256)S(1)} %add_rsqrt_fusion.3) | copy-start | bytes 3076 | tf_op jit(solution)/shard_map/while/body/eval_jaxpr/cond
  703.1 10.7 slice-start.11
  741.1 5.4 copy-start.1
  751.6 8.6 collective-permute-start.1
  780.1 12.6 %slice-start.10 = ((s8[4718592]{0:T(1024)(128)(4,1)}), s8[4194304]{0:T(1024)(128)(4,1)S(1)}, s32[]{:S(2)}) async-start(s8[4718592]{0:T(1024)(128)(4,1)} %bitcast.202), calls=%async_computation.11 | async-start | bytes 8388608 | tf_op jit(solution)/shard_map/while/body/eval_jaxpr/cond
  780.7 20.1 %copy-start.18 = (f32[256]{0:T(256)}, f32[256]{0:T(256)S(1)}, u32[]{:S(2)}) copy-start(f32[256]{0:T(256)S(1)} %broadcast_multiply_fusion.6) | copy-start | bytes 3076 | tf_op jit(solution)/shard_map/while/body/eval_jaxpr/cond
  780.9 19.9 %copy-start.25 = (f32[256]{0:T(256)}, f32[256]{0:T(256)S(1)}, u32[]{:S(2)}) copy-start(f32[256]{0:T(256)S(1)} %add_rsqrt_fusion.3) | copy-start | bytes 3076 | tf_op jit(solution)/shard_map/while/body/eval_jaxpr/cond
  782.1 10.7 slice-start.11
  830.6 8.5 collective-permute-start.1
  859.0 12.6 %slice-start.10 = ((s8[4718592]{0:T(1024)(128)(4,1)}), s8[4194304]{0:T(1024)(128)(4,1)S(1)}, s32[]{:S(2)}) async-start(s8[4718592]{0:T(1024)(128)(4,1)} %bitcast.202), calls=%async_computation.11 | async-start | bytes 8388608 | tf_op jit(solution)/shard_map/while/body/eval_jaxpr/cond
  859.6 20.1 %copy-start.18 = (f32[256]{0:T(256)}, f32[256]{0:T(256)S(1)}, u32[]{:S(2)}) copy-start(f32[256]{0:T(256)S(1)} %broadcast_multiply_fusion.6) | copy-start | bytes 3076 | tf_op jit(solution)/shard_map/while/body/eval_jaxpr/cond
  859.8 19.9 %copy-start.25 = (f32[256]{0:T(256)}, f32[256]{0:T(256)S(1)}, u32[]{:S(2)}) copy-start(f32[256]{0:T(256)S(1)} %add_rsqrt_fusion.3) | copy-start | bytes 3076 | tf_op jit(solution)/shard_map/while/body/eval_jaxpr/cond
  861.0 10.7 slice-start.11
  909.4 8.5 collective-permute-start.1
  918.4 20.0 %slice-start = ((s8[6291456]{0:T(1024)(128)(4,1)}), s8[2097152]{0:T(1024)(128)(4,1)S(1)}, s32[]{:S(2)}) async-start(s8[6291456]{0:T(1024)(128)(4,1)} %bitcast.185), calls=%async_computation.1 | async-start | bytes 4194304
  925.3 13.0 %slice-start.1 = ((s8[6291456]{0:T(1024)(128)(4,1)}), s8[4194304]{0:T(1024)(128)(4,1)S(1)}, s32[]{:S(2)}) async-start(s8[6291456]{0:T(1024)(128)(4,1)} %bitcast.185), calls=%async_computation.2 | async-start | bytes 8388608
  933.9 12.8 %slice-start.2 = ((s8[6291456]{0:T(1024)(128)(4,1)}), s8[4194304]{0:T(1024)(128)(4,1)S(1)}, s32[]{:S(2)}) async-start(s8[6291456]{0:T(1024)(128)(4,1)} %bitcast.191), calls=%async_computation.3 | async-start | bytes 8388608
  938.3 8.4 slice-start.3
  1154.4 7.2 slice-start.6
  1154.4 5.6 copy-start.16
  1154.4 7.2 slice-start.7
  1160.0 6.6 slice-start.4
  (101 other events, 246.6 us)
Sparse Core Ops, SparseCore 0:
  955.4 198.9 all-reduce.3
where the time goes:
time: 1190 us; the launch traced here: 1180 us
  waiting for transfers between devices  473 us (40%)
  matrix products  248 us (21%)
  other arithmetic  148 us (12%)
  local copies, waits for them, and re-layouts  141 us (12%)
  starting transfers between devices  99.7 us (8%)
  blocking collectives  36.3 us (3%)
  loops' own time  17.7 us (1%)
  between operations  14.4 us (1%)
    ppermute x14, waiting for transfers between devices, passed_along(): lax.ppermute(value, axis, [(source, source + steps) for source in range(f...  331 us
    psum x1, waiting for transfers between devices, local(): lax.psum(attend_w.astype(jnp.bfloat16), 'dp').astype(jnp.float32)  143 us
    ppermute x14, starting transfers between devices, passed_along(): lax.ppermute(value, axis, [(source, source + steps) for source in range(f...  99.7 us
    dot_general x8, matrix products, section_forward(): jnp.dot(active, reduce_weight, preferred_element_type=jnp.float32)  57.9 us
    dot_general x4, matrix products, section_forward(): jnp.dot(first_low, expand_weight, preferred_element_type=jnp.float32)  42.5 us
    dot_general x16, matrix products, times_t(): lax.dot_general(left, right, (((1,), (1,)), ((), ())), preferred_element_...  37.6 us
    psum x1, blocking collectives, local(): lax.psum(attend_b.astype(jnp.bfloat16), 'dp').astype(jnp.float32)  36.3 us
    dynamic_update_slice x20, other arithmetic, absorb(): lax.dynamic_update_index_in_dim(buffer, piece, picked, 0)  34.2 us
  transfers between devices with their start and end apart: 15, of which 15 were waited for; matrix products, arithmetic and copies ran while one was open for 2% of the time, Pallas kernels for 0%

commit v1 on v0

v1 whole, which is shorter than its diff:
```python
import functools

import jax
import jax.numpy as jnp
from jax import lax
from jax.experimental import pallas as pl
from jax.experimental.pallas import tpu as pltpu
from jax.sharding import PartitionSpec as P

HEADS = 12
GROUP = 2
BLOCK = 32
CHUNK = 512
epsilon = 1e-05
neg_large = -1000000000.0
MESH = pl.DeviceIdType.MESH
f32 = jnp.float32
bf16 = jnp.bfloat16


def nn(left, right):
    return jnp.dot(left, right, preferred_element_type=f32)


def nt(left, right):
    return lax.dot_general(left, right, (((1,), (1,)), ((), ())), preferred_element_type=f32)


def tn(left, right):
    return lax.dot_general(left, right, (((0,), (0,)), ((), ())), preferred_element_type=f32)


def gelu_pair(x):
    z = jnp.abs(x) * 0.7071067811865476
    t = 1.0 / (1.0 + 0.3275911 * z)
    e = jnp.exp(-0.5 * (x * x))
    poly = t * (0.127414796 + t * (-0.142248368 + t * (0.7107068705 + t * (-0.7265760135 + t * 0.5307027145))))
    tail = poly * e
    phi = jnp.where(x >= 0, 1.0 - tail, tail)
    return x * phi, phi + (x * 0.3989422804014327) * e


def fold(v):
    rows, cols = v.shape
    return jnp.sum(v.reshape(rows // 8, 8, cols), 0)


def pipeline_kernel(
    micro,
    x_any, ct_any, valid, aw, ow, ew, rw, ab, ob, g1, s1, eb, rb, g2, s2,
    y_out, gin_out, h_out, ctx_out, low_out, act_out, gred_out, gexp_out, gatt_out, gproj_out, sums,
    h_ref, g_ref, y_ref, gb_ref, qkv, shares, gp, n1, r1, n2, r2,
    ctx, low, act, gred, gexp, gatt, gproj, gin, acc, mid,
    h_sem, g_sem, ysend_sem, yrecv_sem, gsend_sem, grecv_sem, y_sem, hs_sem,
    ctx_sem, low_sem, act_sem, gred_sem, gexp_sem, gatt_sem, gproj_sem, gin_sem,
):
    stage = lax.axis_index("pipe")
    count = lax.axis_size("pipe")
    last = count - 1
    slots = valid.shape[2]
    rows = h_ref.shape[1]
    groups = rows // slots
    width = h_ref.shape[2]
    hidden = ew.shape[1]
    pairs = width // 128
    before = jnp.maximum(stage - 1, 0)
    after = jnp.minimum(stage + 1, last)

    def send_y(m):
        return pltpu.make_async_remote_copy(
            src_ref=y_ref.at[m], dst_ref=h_ref.at[m], send_sem=ysend_sem.at[m], recv_sem=yrecv_sem.at[m],
            device_id={"pipe": after}, device_id_type=MESH)

    def send_g(m):
        return pltpu.make_async_remote_copy(
            src_ref=gb_ref.at[m], dst_ref=g_ref.at[m], send_sem=gsend_sem.at[m], recv_sem=grecv_sem.at[m],
            device_id={"pipe": before}, device_id_type=MESH)

    def load_h(m):
        return pltpu.make_async_copy(x_any.at[pl.ds(m * rows, rows)], h_ref.at[m], h_sem.at[m])

    def load_g(m):
        return pltpu.make_async_copy(ct_any.at[pl.ds(m * rows, rows)], g_ref.at[m], g_sem.at[m])

    def store(src, dst, sem, m, slot):
        return pltpu.make_async_copy(src.at[slot], dst.at[pl.ds(m * rows, rows)], sem.at[slot])

    @pl.when(stage == 0)
    def _():
        for m in range(micro):
            load_h(m).start()

    @pl.when(stage == last)
    def _():
        for m in range(micro):
            load_g(m).start()

    barrier = pltpu.get_barrier_semaphore()

    @pl.when(stage > 0)
    def _():
        pl.semaphore_signal(barrier, inc=1, device_id={"pipe": before}, device_id_type=MESH)

    @pl.when(stage < last)
    def _():
        pl.semaphore_signal(barrier, inc=1, device_id={"pipe": after}, device_id_type=MESH)

    inside = (stage > 0) & (stage < last)

    @pl.when(inside)
    def _():
        pl.semaphore_wait(barrier, 2)

    @pl.when(jnp.logical_not(inside))
    def _():
        pl.semaphore_wait(barrier, 1)

    sums[...] = jnp.zeros_like(sums)
    lane = lax.broadcasted_iota(jnp.int32, (slots, 128), 1)
    first_half = lane < 64

    def stack(v):
        zero = jnp.zeros_like(v)
        return jnp.concatenate([jnp.where(first_half, v, zero), jnp.where(first_half, zero, v)], 0)

    def unstack(v):
        return jnp.where(first_half, v[:slots], v[slots:])

    o_g2, o_s2, o_rb = 0, width, 2 * width
    o_eb = 3 * width
    o_g1 = o_eb + hidden
    o_s1 = o_g1 + width
    o_ob = o_s1 + width
    o_q = o_ob + width
    o_v = o_q + width

    staged_f = ((ctx, ctx_out, ctx_sem), (low, low_out, low_sem), (act, act_out, act_sem))
    staged_b = ((gred, gred_out, gred_sem), (gexp, gexp_out, gexp_sem), (gatt, gatt_out, gatt_sem),
                (gproj, gproj_out, gproj_sem), (gin, gin_out, gin_sem))

    def forward(m):
        slot = lax.rem(m, 2)

        @pl.when(stage == 0)
        def _():
            load_h(m).wait()

        @pl.when(stage > 0)
        def _():
            send_y(m).wait_recv()

        store(h_ref, h_out, hs_sem, m, m).start()

        @pl.when(m >= 2)
        def _():
            for src, dst, sem in staged_f:
                store(src, dst, sem, m - 2, slot).wait()

        h = h_ref[m]
        for c in range(0, 3 * width, 256):
            p = nn(h, aw[:, c:c + 256]) + ab[:, c:c + 256]
            if c < width:
                p = p * 0.125
            qkv[m, :, c:c + 256] = p.astype(bf16)
        for g in range(groups):
            ok = valid[m * groups + g] > 0
            rs = slice(g * slots, (g + 1) * slots)
            for p in range(pairs):
                q = qkv[m, rs, p * 128:(p + 1) * 128]
                k = qkv[m, rs, width + p * 128:width + (p + 1) * 128]
                v = qkv[m, rs, 2 * width + p * 128:2 * width + (p + 1) * 128]
                s = nt(stack(q), k)
                s = jnp.where(ok, s, neg_large)
                e = jnp.exp(s - jnp.max(s, -1, keepdims=True))
                sh = (e * (1.0 / jnp.sum(e, -1, keepdims=True))).astype(bf16)
                shares[m, g * pairs + p] = sh
                ctx[slot, rs, p * 128:(p + 1) * 128] = unstack(nn(sh, v)).astype(bf16)
        store(ctx, ctx_out, ctx_sem, m, slot).start()
        c_all = ctx[slot]
        for c in range(0, width, 256):
            acc[:, c:c + 256] = nn(c_all, ow[:, c:c + 256]) + ob[:, c:c + 256]
        for b in range(0, rows, BLOCK):
            bs = slice(b, b + BLOCK)
            v = acc[bs, :] + h_ref[m, bs, :].astype(f32)
            centre = v - jnp.mean(v, -1, keepdims=True)
            inv = lax.rsqrt(jnp.mean(centre * centre, -1, keepdims=True) + epsilon)
            normed = centre * inv
            out = normed * g1[...] + s1[...]
            n1[m, bs, :] = normed.astype(bf16)
            r1[m, bs, :] = jnp.broadcast_to(inv, (BLOCK, 128))
            mid[bs, :] = out
            low[slot, bs, :] = out.astype(bf16)
        store(low, low_out, low_sem, m, slot).start()
        l_all = low[slot]
        for c in range(0, hidden, CHUNK):
            x = nn(l_all, ew[:, c:c + CHUNK]) + eb[:, c:c + CHUNK]
            a, d = gelu_pair(x)
            act[slot, :, c:c + CHUNK] = a.astype(bf16)
            gp[m, :, c:c + CHUNK] = d.astype(bf16)
        store(act, act_out, act_sem, m, slot).start()
        a_all = act[slot]
        for c in range(0, width, 256):
            acc[:, c:c + 256] = nn(a_all, rw[:, c:c + 256]) + rb[:, c:c + 256]
        for b in range(0, rows, BLOCK):
            bs = slice(b, b + BLOCK)
            v = acc[bs, :] + mid[bs, :]
            centre = v - jnp.mean(v, -1, keepdims=True)
            inv = lax.rsqrt(jnp.mean(centre * centre, -1, keepdims=True) + epsilon)
            normed = centre * inv
            n2[m, bs, :] = normed.astype(bf16)
            r2[m, bs, :] = jnp.broadcast_to(inv, (BLOCK, 128))
            y_ref[m, bs, :] = (normed * g2[...] + s2[...]).astype(bf16)

        @pl.when(stage < last)
        def _():
            send_y(m).start()

        store(y_ref, y_out, y_sem, m, m).start()

    def norm_back(grad, normed, inv, gain):
        scaled = grad * gain
        return inv * (scaled - jnp.mean(scaled, -1, keepdims=True)
                      - normed * jnp.mean(scaled * normed, -1, keepdims=True))

    def backward(m):
        slot = lax.rem(m, 2)

        @pl.when(stage == last)
        def _():
            load_g(m).wait()

        @pl.when(stage < last)
        def _():
            send_g(m).wait_recv()

        @pl.when(m >= 2)
        def _():
            for src, dst, sem in staged_b:
                store(src, dst, sem, m - 2, slot).wait()

        for b in range(0, rows, BLOCK):
            bs = slice(b, b + BLOCK)
            go = g_ref[m, bs, :].astype(f32)
            normed = n2[m, bs, :].astype(f32)
            mix = norm_back(go, normed, r2[m, bs, 0:1], g2[...])
            mid[bs, :] = mix
            gred[slot, bs, :] = mix.astype(bf16)
            sums[:, o_g2:o_g2 + width] += fold(go * normed)
            sums[:, o_s2:o_s2 + width] += fold(go)
            sums[:, o_rb:o_rb + width] += fold(mix)
        store(gred, gred_out, gred_sem, m, slot).start()
        r_all = gred[slot]
        for c in range(0, hidden, CHUNK):
            ge = nt(r_all, rw[c:c + CHUNK, :]) * gp[m, :, c:c + CHUNK].astype(f32)
            gexp[slot, :, c:c + CHUNK] = ge.astype(bf16)
            sums[:, o_eb + c:o_eb + c + CHUNK] += fold(ge)
        store(gexp, gexp_out, gexp_sem, m, slot).start()
        e_all = gexp[slot]
        for c in range(0, width, 256):
            acc[:, c:c + 256] = nt(e_all, ew[c:c + 256, :])
        for b in range(0, rows, BLOCK):
            bs = slice(b, b + BLOCK)
            gf = acc[bs, :] + mid[bs, :]
            normed = n1[m, bs, :].astype(f32)
            gm = norm_back(gf, normed, r1[m, bs, 0:1], g1[...])
            mid[bs, :] = gm
            gatt[slot, bs, :] = gm.astype(bf16)
            sums[:, o_g1:o_g1 + width] += fold(gf * normed)
            sums[:, o_s1:o_s1 + width] += fold(gf)
            sums[:, o_ob:o_ob + width] += fold(gm)
        store(gatt, gatt_out, gatt_sem, m, slot).start()
        t_all = gatt[slot]
        for c in range(0, width, 256):
            gc_all = nt(t_all, ow[c:c + 256, :]).astype(bf16)
            for g in range(groups):
                rs = slice(g * slots, (g + 1) * slots)
                for half in range(2):
                    p = c // 128 + half
                    q = qkv[m, rs, p * 128:(p + 1) * 128]
                    k = qkv[m, rs, width + p * 128:width + (p + 1) * 128]
                    v = qkv[m, rs, 2 * width + p * 128:2 * width + (p + 1) * 128]
                    shb = shares[m, g * pairs + p]
                    sh = shb.astype(f32)
                    gc2 = stack(gc_all[rs, half * 128:(half + 1) * 128])
                    gs = nt(gc2, v)
                    gv = tn(shb, gc2)
                    gsc = (sh * (gs - jnp.sum(gs * sh, -1, keepdims=True))).astype(bf16)
                    gq = unstack(nn(gsc, k)) * 0.125
                    gk = tn(gsc, stack(q))
                    gproj[slot, rs, p * 128:(p + 1) * 128] = gq.astype(bf16)
                    gproj[slot, rs, width + p * 128:width + (p + 1) * 128] = gk.astype(bf16)
                    gproj[slot, rs, 2 * width + p * 128:2 * width + (p + 1) * 128] = gv.astype(bf16)
                    sums[:, o_q + p * 128:o_q + (p + 1) * 128] += fold(gq)
                    sums[:, o_v + p * 128:o_v + (p + 1) * 128] += fold(gv)
        store(gproj, gproj_out, gproj_sem, m, slot).start()
        p_all = gproj[slot]
        for c in range(0, width, 256):
            gi = nt(p_all, aw[c:c + 256, :]) + mid[:, c:c + 256]
            gin[slot, :, c:c + 256] = gi
            gb_ref[m, :, c:c + 256] = gi.astype(bf16)

        @pl.when(stage > 0)
        def _():
            send_g(m).start()

        store(gin, gin_out, gin_sem, m, slot).start()

    def tick(i, carry):
        @pl.when(i < micro)
        def _():
            forward(i)

        j = i - (last - stage)

        @pl.when((j >= 0) & (j < micro))
        def _():
            backward(j)

        return carry

    lax.fori_loop(0, micro + last, tick, 0)

    for m in range(micro):
        store(h_ref, h_out, hs_sem, m, m).wait()
        store(y_ref, y_out, y_sem, m, m).wait()

        @pl.when(stage < last)
        def _():
            send_y(m).wait_send()

        @pl.when(stage > 0)
        def _():
            send_g(m).wait_send()

    for m in range(max(0, micro - 2), micro):
        for src, dst, sem in staged_f + staged_b:
            store(src, dst, sem, m, m % 2).wait()


def run_pipeline(rows_in, tangents, valid, weights, vectors):
    total, width = rows_in.shape
    slots = valid.shape[2]
    rows = GROUP * slots
    micro = total // rows
    aw, ow, ew, rw = weights
    hidden = ew.shape[1]
    pairs = width // 128
    wide = 3 * width
    sum_width = 8 * width + hidden
    hbm = pl.BlockSpec(memory_space=pl.ANY)
    vmem = pl.BlockSpec(memory_space=pltpu.VMEM)
    dma = pltpu.SemaphoreType.DMA
    shape = jax.ShapeDtypeStruct
    flops = 4 * total * (4 * width * width + 2 * width * hidden)
    return pl.pallas_call(
        functools.partial(pipeline_kernel, micro),
        out_shape=(
            shape((total, width), bf16), shape((total, width), f32), shape((total, width), bf16),
            shape((total, width), bf16), shape((total, width), bf16), shape((total, hidden), bf16),
            shape((total, width), bf16), shape((total, hidden), bf16), shape((total, width), bf16),
            shape((total, wide), bf16), shape((8, sum_width), f32),
        ),
        in_specs=[hbm, hbm] + [vmem] * 13,
        out_specs=(hbm,) * 10 + (vmem,),
        scratch_shapes=[
            pltpu.VMEM((micro, rows, width), bf16),
            pltpu.VMEM((micro, rows, width), bf16),
            pltpu.VMEM((micro, rows, width), bf16),
            pltpu.VMEM((micro, rows, width), bf16),
            pltpu.VMEM((micro, rows, wide), bf16),
            pltpu.VMEM((micro, GROUP * pairs, 2 * slots, slots), bf16),
            pltpu.VMEM((micro, rows, hidden), bf16),
            pltpu.VMEM((micro, rows, width), bf16),
            pltpu.VMEM((micro, rows, 128), f32),
            pltpu.VMEM((micro, rows, width), bf16),
            pltpu.VMEM((micro, rows, 128), f32),
            pltpu.VMEM((2, rows, width), bf16),
            pltpu.VMEM((2, rows, width), bf16),
            pltpu.VMEM((2, rows, hidden), bf16),
            pltpu.VMEM((2, rows, width), bf16),
            pltpu.VMEM((2, rows, hidden), bf16),
            pltpu.VMEM((2, rows, width), bf16),
            pltpu.VMEM((2, rows, wide), bf16),
            pltpu.VMEM((2, rows, width), f32),
            pltpu.VMEM((rows, width), f32),
            pltpu.VMEM((rows, width), f32),
        ] + [dma((micro,))] * 8 + [dma((2,))] * 8,
        compiler_params=pltpu.CompilerParams(
            collective_id=0, has_side_effects=True, vmem_limit_bytes=63 * 1024 * 1024),
        cost_estimate=pl.CostEstimate(flops=flops, bytes_accessed=40_000_000, transcendentals=total * hidden),
    )(rows_in, tangents, valid, aw, ow, ew, rw, *vectors)


def outer_sum(left, right):
    return tn(left, right)


def local(
    layer_input, lengths, regions, cotangent,
    attend_weight, attend_bias, output_weight, output_bias, first_gain, first_shift,
    expand_weight, expand_bias, reduce_weight, reduce_bias, second_gain, second_shift,
):
    seqs, slots, width = layer_input.shape
    hidden = expand_weight.shape[2]
    total = seqs * slots
    positions = jnp.arange(slots, dtype=jnp.int32)
    valid = ((positions[None, :] < lengths[:, None]) | (regions == 1)).astype(f32)[:, None, :]
    bias = attend_bias.astype(f32)
    bias = jnp.concatenate([bias[:, :width], jnp.zeros((1, width), f32), bias[:, width:]], 1)
    vectors = (bias,) + tuple(
        v.astype(f32)
        for v in (output_bias, first_gain, first_shift, expand_bias, reduce_bias, second_gain, second_shift)
    )
    weights = (attend_weight[0], output_weight[0], expand_weight[0], reduce_weight[0])
    y, gin, h, ctx, low, act, gred, gexp, gatt, gproj, sums = run_pipeline(
        layer_input.reshape(total, width), cotangent.reshape(total, width), valid, weights, vectors)

    def reduced(v):
        return lax.psum(v.astype(bf16), "dp").astype(f32)

    rw_g = reduced(outer_sum(act, gred))
    ew_g = reduced(outer_sum(low, gexp))
    ow_g = reduced(outer_sum(ctx, gatt))
    aw_g = reduced(outer_sum(h, gproj))
    flat = reduced(jnp.sum(sums, 0))[None]
    at = [0, width, 2 * width, 3 * width, 3 * width + hidden]
    o1 = at[4]
    return (
        y.reshape(1, seqs, slots, width),
        gin.reshape(1, seqs, slots, width),
        aw_g[None],
        flat[:, o1 + 3 * width:],
        ow_g[None],
        flat[:, o1 + 2 * width:o1 + 3 * width],
        flat[:, o1:o1 + width],
        flat[:, o1 + width:o1 + 2 * width],
        ew_g[None],
        flat[:, 3 * width:o1],
        rw_g[None],
        flat[:, 2 * width:3 * width],
        flat[:, :width],
        flat[:, width:2 * width],
    )


def solution(mesh):
    rows = P("dp", None, None)
    cube = P("pipe", None, None)
    flat = P("pipe", None)
    grads = P("pipe", "dp", None, None)
    return jax.shard_map(
        local,
        mesh=mesh,
        in_specs=(rows, P("dp"), P("dp", None), rows, cube, flat, cube, flat, flat, flat, cube, flat, cube, flat, flat, flat),
        out_specs=(grads, grads, cube, flat, cube, flat, flat, flat, cube, flat, cube, flat, flat, flat),
        check_vma=False,
    )
```

time: 1190 us -> 470 us (0.39)
  waiting for transfers between devices: 473 us -> 163 us
  matrix products: 248 us -> 23.8 us
  Pallas kernels: 0 us -> 201 us
  local copies, waits for them, and re-layouts: 141 us -> 8.02 us
  other arithmetic: 148 us -> 28 us
  starting transfers between devices: 99.7 us -> 0.04 us
  loops' own time: 17.7 us -> 0 us
    ppermute x14 -> x0, waiting for transfers between devices: 331 us -> none  [passed_along(): lax.ppermute(value, axis, [(source, source + steps) for source in range(f...]
    dot_general x72 -> x4, matrix products: 231 us -> 23.8 us  [tn(): lax.dot_general(left, right, (((0,), (0,)), ((), ())), preferred_element_...]
    pallas_call x0 -> x1, Pallas kernels: none -> 201 us  [run_pipeline(): pl.pallas_call(functools.partial(pipeline_kernel, micro), out_shape=(shap...]
    ppermute x14 -> x0, starting transfers between devices: 99.7 us -> none  [passed_along(): lax.ppermute(value, axis, [(source, source + steps) for source in range(f...]
    convert_element_type x90 -> x7, other arithmetic: 54.7 us -> 8.9 us  [local(): v.astype(f32)]
    dynamic_update_slice x24 -> x0, other arithmetic: 41.5 us -> none  [the longest x20 34.2 us: absorb(): lax.dynamic_update_index_in_dim(buffer, piece, picked, 0)]
    another operation x22 -> x0, local copies, waits for them, and re-layouts: 24.7 us -> none
    reduce_sum x29 -> x1, other arithmetic: 20.5 us -> 0.08 us  [local(): flat = reduced(jnp.sum(sums, 0))[None]]
  transfers between devices with their start and end apart: 15 -> 1, of which waited for: 15 -> 1; matrix products, arithmetic and copies ran while one was open for 2% -> 0% of each run, Pallas kernels for 0% -> 0%
where the time goes in v1:
time: 470 us; the launch traced here: 468 us
  Pallas kernels  201 us (43%)
  waiting for transfers between devices  163 us (35%)
  blocking collectives  30.9 us (7%)
  other arithmetic  28 us (6%)
  matrix products  23.8 us (5%)
  between operations  14.1 us (3%)
  local copies, waits for them, and re-layouts  8.02 us (2%)
    pallas_call x1, Pallas kernels, run_pipeline(): pl.pallas_call(functools.partial(pipeline_kernel, micro), out_shape=(shap...  201 us
    psum x1, waiting for transfers between devices, reduced(): return lax.psum(v.astype(bf16), 'dp').astype(f32)  163 us
    psum x1, blocking collectives, reduced(): return lax.psum(v.astype(bf16), 'dp').astype(f32)  30.9 us
    dot_general x4, matrix products, tn(): lax.dot_general(left, right, (((0,), (0,)), ((), ())), preferred_element_...  23.8 us
  transfers between devices with their start and end apart: 1, of which 1 were waited for; matrix products, arithmetic and copies ran while one was open for 0% of the time, Pallas kernels for 0%

profile of v1, /device:TPU:1, one launch (start us, length us, event | category | flops | bytes accessed | tf_op | source)
XLA Modules:
  0.0 468.4 jit_solution(4578666108358283909)
XLA Ops:
  7.2 0.0 all-reduce.3.cloned.1.call-start
  7.2 0.7 fusion.8
  7.9 1.3 convert_element_type.49.eb
  9.3 1.3 convert_element_type.46.ob
  10.5 1.3 convert_element_type.47.g1
  11.8 1.3 convert_element_type.48.s1
  13.0 1.3 convert_element_type.50.rb
  14.3 1.3 convert_element_type.51.g2
  15.6 1.3 convert_element_type.52.s2
  16.9 1.4 fusion.6
  18.2 0.6 fusion.4.ab
  18.8 200.6 %shard_map.263 = (bf16[1024,768]{1,0:T(8,128)(2,1)}, f32[1024,768]{1,0:T(8,128)}, bf16[1024,768]{1,0:T(8,128)(2,1)}, bf16[1024,768]{1,0:T(8,128)(2,1)}, bf16[102...) custom-call(bf16[1024,768]{1,0:T(8,128)(2,1)} %bitcast.31, ...), custom_call_target="tpu_custom_call" | custom-call | flops 28991029248 | bytes 40000000 | tf_op jit(solution)/shard_map/pallas_call | solution.py:355
  219.4 0.0 copy-start.6
  219.4 0.0 copy-start.10
  219.4 9.3 %fusion.2 = bf16[1,3072,768]{2,1,0:T(8,128)(2,1)} fusion(bf16[1024,3072]{1,0:T(8,128)(2,1)} %get-tuple-element.34, bf16[1024,768]{1,0:T(8,128)(2,1)} %get-tuple-element.35), kind=kOutput, calls=%fused_computation.5 | convolution fusion | flops 4834197504 | bytes 12582912 | tf_op jit(solution)/shard_map/dot_general | solution.py:30
  228.7 0.0 copy-done.6
  228.7 0.0 copy-done.10
  228.7 0.0 copy-start.8
  228.7 0.0 copy-start.9
  228.7 6.8 %fusion.1 = bf16[1,768,3072]{2,1,0:T(8,128)(2,1)} fusion(bf16[1024,768]{1,0:T(8,128)(2,1)S(1)} %copy-done.10, bf16[1024,3072]{1,0:T(8,128)(2,1)S(1)} %copy-done.6), kind=kOutput, calls=%fused_computation.4 | convolution fusion | flops 4834197504 | bytes 12582912 | tf_op jit(solution)/shard_map/dot_general | solution.py:30
  235.5 0.0 copy-done.8
  235.5 0.0 copy-done.9
  235.5 0.0 copy-start.7
  235.5 0.0 copy-start.11
  235.5 2.5 fusion.3
  238.0 0.0 copy-done.7
  238.0 0.8 copy-done.11
  238.8 5.3 %fusion = bf16[1,768,2304]{2,1,0:T(8,128)(2,1)} fusion(bf16[1024,768]{1,0:T(8,128)(2,1)S(1)} %copy-done.11, bf16[1024,2304]{1,0:T(8,128)(2,1)S(1)} %copy-done.7), kind=kOutput, calls=%fused_computation.3 | convolution fusion | flops 3625648128 | bytes 9830400 | tf_op jit(solution)/shard_map/dot_general | solution.py:30
  244.1 0.0 copy-start.5
  244.1 0.0 all-reduce.3.cloned.1.call-update
  244.1 0.9 copy-done.5
  245.0 0.1 reduce_sum.9
  245.1 30.9 %psum.36 = bf16[1,9216]{1,0:T(2,128)(2,1)S(1)} all-reduce(bf16[1,9216]{1,0:T(2,128)(2,1)S(1)} %broadcast_in_dim.45), channel_id=1, replica_groups=mesh['dp'=8,'pipe'=4] {'dp'}, use_global_device_ids=true, to_apply=%region_2.0 | all-reduce | flops 9216 | bytes 36864 | tf_op jit(solution)/shard_map/psum | solution.py:419
  276.1 0.6 slice.46
  276.7 0.6 slice.42
  277.3 0.6 fusion.7
  277.9 162.9 %all-reduce.3.cloned.1.call-done = (bf16[1,768,2304]{2,1,0:T(8,128)(2,1)}, bf16[1,768,768]{2,1,0:T(8,128)(2,1)}, bf16[1,768,3072]{2,1,0:T(8,128)(2,1)}, bf16[1,3072,768]{2,1,0:T(8,128)(2,1)}) async-done(((bf16[1,768,2304]{2,1,0:T(8,128)(2,1)}, bf16[1,768,768]{2,1,0:T(8,128)(2,1)}, bf16[1,768,3072]{2,1,0:T(8,128)(2,1)}, bf16[1,3072,768]{2,1,0:T(8,128)(2,1)}), (bf16[1,768,2304]{2,1,0:T(8,128)(2,1)}, ...) | async-done | bytes 14155792 | tf_op jit(solution)/shard_map/psum | solution.py:419
  440.7 7.5 %broadcast_in_dim.50 = f32[1,768,3072]{2,1,0:T(8,128)} convert(bf16[1,768,3072]{2,1,0:T(8,128)(2,1)} %get-tuple-element.38) | non-fusion elementwise | flops 2359296 | bytes 14155776 | tf_op jit(solution)/shard_map/broadcast_in_dim | solution.py:437
  448.3 0.0 copy-done
  448.3 4.5 broadcast_in_dim.52
  452.8 0.0 copy-done.1
  452.8 3.5 broadcast_in_dim.44
  456.2 0.0 copy-done.4
  456.2 1.6 broadcast_in_dim.48
  457.8 0.5 copy-done.3
  458.3 1.1 copy.36
  459.5 0.4 copy-done.2
  459.9 1.7 copy.37
  (8 shorter events, 0.0 us)
Async XLA Ops:
  7.2 433.6 %all-reduce.3.cloned.1.call-start = ((), (), s32[]{:S(2)}) async-start(), calls=%async_computation | async-start | bytes 28311552 | tf_op jit(solution)/shard_map/psum | solution.py:419
  219.4 9.3 %copy-start.6 = (bf16[1024,3072]{1,0:T(8,128)(2,1)S(1)}, bf16[1024,3072]{1,0:T(8,128)(2,1)}, u32[]{:S(2)}) copy-start(bf16[1024,3072]{1,0:T(8,128)(2,1)} %get-tuple-element.33) | copy-start | bytes 18874372
  219.4 9.3 %copy-start.10 = (bf16[1024,768]{1,0:T(8,128)(2,1)S(1)}, bf16[1024,768]{1,0:T(8,128)(2,1)}, u32[]{:S(2)}) copy-start(bf16[1024,768]{1,0:T(8,128)(2,1)} %get-tuple-element.32) | copy-start | bytes 4718596
  228.7 6.8 %copy-start.8 = (bf16[1024,768]{1,0:T(8,128)(2,1)S(1)}, bf16[1024,768]{1,0:T(8,128)(2,1)}, u32[]{:S(2)}) copy-start(bf16[1024,768]{1,0:T(8,128)(2,1)} %get-tuple-element.30) | copy-start | bytes 4718596
  228.7 6.8 %copy-start.9 = (bf16[1024,768]{1,0:T(8,128)(2,1)S(1)}, bf16[1024,768]{1,0:T(8,128)(2,1)}, u32[]{:S(2)}) copy-start(bf16[1024,768]{1,0:T(8,128)(2,1)} %get-tuple-element.31) | copy-start | bytes 4718596
  235.5 2.5 copy-start.7
  235.5 3.3 copy-start.11
  244.1 1.0 copy-start.5
  440.7 7.5 %copy-start = (bf16[1,3072,768]{2,1,0:T(8,128)(2,1)S(1)}, bf16[1,3072,768]{2,1,0:T(8,128)(2,1)}, u32[]{:S(2)}) copy-start(bf16[1,3072,768]{2,1,0:T(8,128)(2,1)} %get-tuple-element.39) | copy-start | bytes 14155780
  448.3 4.5 copy-start.1
  452.8 3.5 copy-start.4
  456.2 2.1 copy-start.3
  456.2 3.6 copy-start.2
Sparse Core Ops, SparseCore 0:
  244.2 196.4 all-reduce.2

commit v2 on v1

--- a/solution.py
+++ b/solution.py
@@ -47,8 +47,9 @@
 
 def pipeline_kernel(
     micro,
-    x_any, ct_any, valid, aw, ow, ew, rw, ab, ob, g1, s1, eb, rb, g2, s2,
+    x_any, ct_any, lengths, regions, aw, ow, ew, rw, ab_in, ob_in, g1_in, s1_in, eb_in, rb_in, g2_in, s2_in,
     y_out, gin_out, h_out, ctx_out, low_out, act_out, gred_out, gexp_out, gatt_out, gproj_out, sums,
+    ab, ob, g1, s1, eb, rb, g2, s2,
     h_ref, g_ref, y_ref, gb_ref, qkv, shares, gp, n1, r1, n2, r2,
     ctx, low, act, gred, gexp, gatt, gproj, gin, acc, mid,
     h_sem, g_sem, ysend_sem, yrecv_sem, gsend_sem, grecv_sem, y_sem, hs_sem,
@@ -57,7 +58,7 @@
     stage = lax.axis_index("pipe")
     count = lax.axis_size("pipe")
     last = count - 1
-    slots = valid.shape[2]
+    slots = regions.shape[1]
     rows = h_ref.shape[1]
     groups = rows // slots
     width = h_ref.shape[2]
@@ -116,6 +117,12 @@
         pl.semaphore_wait(barrier, 1)
 
     sums[...] = jnp.zeros_like(sums)
+    ab[:, :width] = ab_in[:, :width].astype(f32)
+    ab[:, width:2 * width] = jnp.zeros((1, width), f32)
+    ab[:, 2 * width:] = ab_in[:, width:].astype(f32)
+    for dst, src in ((ob, ob_in), (g1, g1_in), (s1, s1_in), (eb, eb_in), (rb, rb_in), (g2, g2_in), (s2, s2_in)):
+        dst[...] = src[...].astype(f32)
+    position = lax.broadcasted_iota(jnp.int32, (1, slots), 1)
     lane = lax.broadcasted_iota(jnp.int32, (slots, 128), 1)
     first_half = lane < 64
 
@@ -163,7 +170,8 @@
                 p = p * 0.125
             qkv[m, :, c:c + 256] = p.astype(bf16)
         for g in range(groups):
-            ok = valid[m * groups + g] > 0
+            seq = m * groups + g
+            ok = (position < lengths[seq]) | (regions[pl.ds(seq, 1), :] == 1)
             rs = slice(g * slots, (g + 1) * slots)
             for p in range(pairs):
                 q = qkv[m, rs, p * 128:(p + 1) * 128]
@@ -337,9 +345,9 @@
             store(src, dst, sem, m, m % 2).wait()
 
 
-def run_pipeline(rows_in, tangents, valid, weights, vectors):
+def run_pipeline(rows_in, tangents, lengths, regions, weights, vectors):
     total, width = rows_in.shape
-    slots = valid.shape[2]
+    slots = regions.shape[1]
     rows = GROUP * slots
     micro = total // rows
     aw, ow, ew, rw = weights
@@ -360,9 +368,9 @@
             shape((total, width), bf16), shape((total, hidden), bf16), shape((total, width), bf16),
             shape((total, wide), bf16), shape((8, sum_width), f32),
         ),
-        in_specs=[hbm, hbm] + [vmem] * 13,
+        in_specs=[hbm, hbm, pl.BlockSpec(memory_space=pltpu.SMEM)] + [vmem] * 13,
         out_specs=(hbm,) * 10 + (vmem,),
-        scratch_shapes=[
+        scratch_shapes=[pltpu.VMEM((1, n), f32) for n in (wide, width, width, width, hidden, width, width, width)] + [
             pltpu.VMEM((micro, rows, width), bf16),
             pltpu.VMEM((micro, rows, width), bf16),
             pltpu.VMEM((micro, rows, width), bf16),
@@ -388,11 +396,283 @@
         compiler_params=pltpu.CompilerParams(
             collective_id=0, has_side_effects=True, vmem_limit_bytes=63 * 1024 * 1024),
         cost_estimate=pl.CostEstimate(flops=flops, bytes_accessed=40_000_000, transcendentals=total * hidden),
-    )(rows_in, tangents, valid, aw, ow, ew, rw, *vectors)
-
-
-def outer_sum(left, right):
-    return tn(left, right)
+    )(rows_in, tangents, lengths, regions, aw, ow, ew, rw, *vectors)
+
+
+def sum_kernel(
+    dp, act_any, gred_any, low_any, gexp_any, h_any, gproj_any, ctx_any, gatt_any, sums_in,
+    total, vector,
+    part, left, right, vec_in, *rest,
+):
+    steps = dp.bit_length() - 1
+    plane = steps - 1
+    landed = rest[:steps]
+    left_sem, right_sem, send_sem, recv_sem, vsend_sem, vrecv_sem = rest[steps:]
+    units, rows, cols = part.shape
+    me = lax.axis_index("dp")
+    hid_blocks = act_any.shape[1] // cols
+    wide_blocks = gproj_any.shape[1] // cols
+    sources = (
+        [(act_any, k, gred_any, 0) for k in range(hid_blocks)]
+        + [(low_any, 0, gexp_any, k) for k in range(hid_blocks)]
+        + [(h_any, 0, gproj_any, k) for k in range(wide_blocks)]
+        + [(ctx_any, 0, gatt_any, 0)]
+    )
+
+    def bit_of(mask):
+        return lax.rem(me // mask, 2)
+
+    def masks_of(step):
+        if step == 0:
+            return 1, 1
+        return 2 ** (1 + (step - 1) % plane), 2 ** (1 + (step - 1 + plane // 2) % plane)
+
+    def place(unit, step):
+        parity = lax.rem(unit, 2)
+        first, second = masks_of(step)
+        mask = first + parity * (second - first)
+        bit = bit_of(first) + parity * (bit_of(second) - bit_of(first))
+        return bit, me + mask * (1 - 2 * bit)
+
+    def base(unit, step):
+        start, size = 0, rows
+        for k in range(step):
+            size = size // 2
+            start = start + place(unit, k)[0] * size
+        return start, size
+
+    def ds(start, size):
+        return pl.ds(pl.multiple_of(start, 16), size)
+
+    def reduce_copy(unit, step):
+        bit, peer = place(unit, step)
+        start, size = base(unit, step)
+        half = size // 2
+        return pltpu.make_async_remote_copy(
+            src_ref=part.at[unit, ds(start + (1 - bit) * half, half)], dst_ref=landed[step].at[unit],
+            send_sem=send_sem.at[step, unit], recv_sem=recv_sem.at[step, unit],
+            device_id={"dp": peer}, device_id_type=MESH)
+
+    def gather_copy(unit, step):
+        peer = place(unit, step)[1]
+        start, size = base(unit, step + 1)
+        where = 2 * steps - 1 - step
+        return pltpu.make_async_remote_copy(
+            src_ref=total.at[unit, ds(start, size)], dst_ref=total.at[unit, ds(start, size)],
+            send_sem=send_sem.at[where, unit], recv_sem=recv_sem.at[where, unit],
+            device_id={"dp": peer}, device_id_type=MESH)
+
+    def gather_arrival(unit, step):
+        bit, peer = place(unit, step)
+        start, size = base(unit, step)
+        half = size // 2
+        where = 2 * steps - 1 - step
+        there = ds(start + (1 - bit) * half, half)
+        return pltpu.make_async_remote_copy(
+            src_ref=total.at[unit, there], dst_ref=total.at[unit, there],
+            send_sem=send_sem.at[where, unit], recv_sem=recv_sem.at[where, unit],
+            device_id={"dp": peer}, device_id_type=MESH)
+
+    def vector_copy(step):
+        peer = me + 2 ** step * (1 - 2 * bit_of(2 ** step))
+        return pltpu.make_async_remote_copy(
+            src_ref=vec_in.at[2 * step], dst_ref=vec_in.at[2 * step + 1],
+            send_sem=vsend_sem.at[step], recv_sem=vrecv_sem.at[step],
+            device_id={"dp": peer}, device_id_type=MESH)
+
+    def loads(k, slot):
+        a, ka, b, kb = sources[k]
+        return (
+            pltpu.make_async_copy(a.at[:, pl.ds(ka * cols, cols)], left.at[slot], left_sem.at[slot]),
+            pltpu.make_async_copy(b.at[:, pl.ds(kb * cols, cols)], right.at[slot], right_sem.at[slot]),
+        )
+
+    for copy in loads(0, 0):
+        copy.start()
+    barrier = pltpu.get_barrier_semaphore()
+    for step in range(steps):
+        peer = me + 2 ** step * (1 - 2 * bit_of(2 ** step))
+        pl.semaphore_signal(barrier, inc=1, device_id={"dp": peer}, device_id_type=MESH)
+    v = jnp.sum(sums_in[...], 0, keepdims=True)
+    lanes = vec_in.shape[2]
+    for r in range(8):
+        vec_in[0, r:r + 1, :] = v[:, r * lanes:(r + 1) * lanes]
+    pl.semaphore_wait(barrier, steps)
+
+    def add(unit, step):
+        start, size = base(unit, step + 1)
+        for b in range(0, size, 96):
+            n = min(96, size - b)
+            rs = ds(start + b, n)
+            s = part[unit, rs, :].astype(f32) + landed[step][unit, b:b + n, :].astype(f32)
+            if step == steps - 1:
+                total[unit, rs, :] = s.astype(bf16)
+            else:
+                part[unit, rs, :] = s.astype(bf16)
+
+    def when_unit(unit, body):
+        @pl.when((unit >= 0) & (unit < units))
+        def _():
+            body(unit)
+
+    def make(unit):
+        for s in range(rows // cols):
+            block = unit * (rows // cols) + s
+            slot = lax.rem(block, 2)
+            for k in range(len(sources)):
+                @pl.when(block == k)
+                def _():
+                    if k + 1 < len(sources):
+                        for copy in loads(k + 1, (k + 1) % 2):
+                            copy.start()
+                    for copy in loads(k, k % 2):
+                        copy.wait()
+            for r in range(0, cols, 256):
+                part[unit, s * cols + r:s * cols + r + 256, :] = tn(left[slot, :, r:r + 256], right[slot]).astype(bf16)
+        reduce_copy(unit, 0).start()
+
+    def reduce_next(step):
+        def body(unit):
+            reduce_copy(unit, step).wait_recv()
+            add(unit, step)
+            if step + 1 < steps:
+                reduce_copy(unit, step + 1).start()
+            else:
+                gather_copy(unit, step).start()
+        return body
+
+    def gather_next(step):
+        def body(unit):
+            gather_arrival(unit, step).wait_recv()
+            if step > 0:
+                gather_copy(unit, step - 1).start()
+        return body
+
+    lag = 0
+    lags = []
+    for step in range(steps):
+        lag += 1 if step == 0 else 2
+        lags.append((lag, reduce_next(step)))
+    for step in reversed(range(steps)):
+        lag += 2
+        lags.append((lag, gather_next(step)))
+
+    def tick(t, carry):
+        when_unit(t, make)
+        for behind, body in lags:
+            when_unit(t - behind, body)
+        for step in range(steps):
+            @pl.when(t == 2 + 2 * step)
+            def _():
+                if step > 0:
+                    vector_copy(step - 1).wait_recv()
+                    vec_in[2 * step] = vec_in[2 * step - 2] + vec_in[2 * step - 1]
+                vector_copy(step).start()
+
+        return carry
+
+    lax.fori_loop(0, units + lag, tick, 0)
+    vector_copy(steps - 1).wait_recv()
+    vector[...] = vec_in[2 * steps - 2] + vec_in[2 * steps - 1]
+
+    def finish(unit, carry):
+        for step in range(steps):
+            reduce_copy(unit, step).wait_send()
+            gather_copy(unit, step).wait_send()
+        return carry
+
+    lax.fori_loop(0, units, finish, 0)
+    for step in range(steps):
+        vector_copy(step).wait_send()
+
+
+def write_kernel(hid_blocks, wide_blocks, total, vector, aw_g, ab_g, ow_g, ob_g, g1_g, s1_g, ew_g, eb_g, rw_g, rb_g, g2_g, s2_g):
+    t = pl.program_id(0)
+    first, second = hid_blocks, 2 * hid_blocks
+    third = second + wide_blocks
+
+    @pl.when(t == 0)
+    def _():
+        piece = vector.shape[1] // 3
+        at = 0
+        for out in (g2_g, s2_g, rb_g, eb_g, g1_g, s1_g, ob_g, ab_g):
+            for k in range(out.shape[1] // piece):
+                r, c = at // 3, at % 3
+                out[:, k * piece:(k + 1) * piece] = vector[r:r + 1, c * piece:(c + 1) * piece]
+                at += 1
+
+    @pl.when(t < first)
+    def _():
+        rw_g[...] = total[...].astype(f32)
+
+    @pl.when((t >= first) & (t < second))
+    def _():
+        ew_g[...] = total[...].astype(f32)
+
+    @pl.when((t >= second) & (t < third))
+    def _():
+        aw_g[...] = total[...].astype(f32)
+
+    @pl.when(t >= third)
+    def _():
+        ow_g[...] = total[...].astype(f32)
+
+
+def run_sums(parts, sums, dp):
+    act, gred, low, gexp, h, gproj, ctx, gatt = parts
+    total_rows, width = h.shape
+    hidden, wide = act.shape[1], gproj.shape[1]
+    hid_blocks, wide_blocks = hidden // width, wide // width
+    blocks = 2 * hid_blocks + wide_blocks + 1
+    steps = dp.bit_length() - 1
+    span = 1
+    while span * width % (16 * dp):
+        span *= 2
+    units, unit_rows = blocks // span, span * width
+    lanes = sums.shape[1] // 8
+    hbm = pl.BlockSpec(memory_space=pl.ANY)
+    vmem = pl.BlockSpec(memory_space=pltpu.VMEM)
+    dma = pltpu.SemaphoreType.DMA
+    shape = jax.ShapeDtypeStruct
+    total, vector = pl.pallas_call(
+        functools.partial(sum_kernel, dp),
+        out_shape=(shape((units, unit_rows, width), bf16), shape((8, lanes), f32)),
+        in_specs=[hbm] * 8 + [vmem],
+        out_specs=(vmem, vmem),
+        scratch_shapes=[
+            pltpu.VMEM((units, unit_rows, width), bf16),
+            pltpu.VMEM((2, total_rows, width), bf16),
+            pltpu.VMEM((2, total_rows, width), bf16),
+            pltpu.VMEM((2 * steps, 8, lanes), f32),
+        ] + [pltpu.VMEM((units, unit_rows // 2 ** (k + 1), width), bf16) for k in range(steps)] + [
+            dma((2,)), dma((2,)), dma((2 * steps, units)), dma((2 * steps, units)), dma((steps,)), dma((steps,)),
+        ],
+        compiler_params=pltpu.CompilerParams(
+            collective_id=1, has_side_effects=True, vmem_limit_bytes=63 * 1024 * 1024),
+    )(act, gred, low, gexp, h, gproj, ctx, gatt, sums)
+
+    def one(count):
+        return shape((1, count), f32), pl.BlockSpec((1, count), lambda t: (0, 0))
+
+    a, b = hid_blocks, 2 * hid_blocks
+    outs = [
+        (shape((width, wide), f32), pl.BlockSpec((width, width), lambda t: (0, jnp.clip(t - b, 0, wide_blocks - 1)))),
+        one(2 * width),
+        (shape((width, width), f32), pl.BlockSpec((width, width), lambda t: (0, 0))),
+        one(width), one(width), one(width),
+        (shape((width, hidden), f32), pl.BlockSpec((width, width), lambda t: (0, jnp.clip(t - a, 0, hid_blocks - 1)))),
+        one(hidden),
+        (shape((hidden, width), f32), pl.BlockSpec((width, width), lambda t: (jnp.clip(t, 0, hid_blocks - 1), 0))),
+        one(width), one(width), one(width),
+    ]
+    return pl.pallas_call(
+        functools.partial(write_kernel, hid_blocks, wide_blocks),
+        grid=(blocks,),
+        out_shape=tuple(o[0] for o in outs),
+        in_specs=[pl.BlockSpec((None, width, width), lambda t: (t, 0, 0)), pl.BlockSpec((8, lanes), lambda t: (0, 0))],
+        out_specs=tuple(o[1] for o in outs),
+        compiler_params=pltpu.CompilerParams(vmem_limit_bytes=60 * 1024 * 1024),
+    )(total.reshape(blocks, width, width), vector)
 
 
 def local(
@@ -401,46 +681,14 @@
     expand_weight, expand_bias, reduce_weight, reduce_bias, second_gain, second_shift,
 ):
     seqs, slots, width = layer_input.shape
-    hidden = expand_weight.shape[2]
     total = seqs * slots
-    positions = jnp.arange(slots, dtype=jnp.int32)
-    valid = ((positions[None, :] < lengths[:, None]) | (regions == 1)).astype(f32)[:, None, :]
-    bias = attend_bias.astype(f32)
-    bias = jnp.concatenate([bias[:, :width], jnp.zeros((1, width), f32), bias[:, width:]], 1)
-    vectors = (bias,) + tuple(
-        v.astype(f32)
-        for v in (output_bias, first_gain, first_shift, expand_bias, reduce_bias, second_gain, second_shift)
-    )
+    vectors = (attend_bias, output_bias, first_gain, first_shift, expand_bias, reduce_bias, second_gain, second_shift)
     weights = (attend_weight[0], output_weight[0], expand_weight[0], reduce_weight[0])
     y, gin, h, ctx, low, act, gred, gexp, gatt, gproj, sums = run_pipeline(
-        layer_input.reshape(total, width), cotangent.reshape(total, width), valid, weights, vectors)
-
-    def reduced(v):
-        return lax.psum(v.astype(bf16), "dp").astype(f32)
-
-    rw_g = reduced(outer_sum(act, gred))
-    ew_g = reduced(outer_sum(low, gexp))
-    ow_g = reduced(outer_sum(ctx, gatt))
-    aw_g = reduced(outer_sum(h, gproj))
-    flat = reduced(jnp.sum(sums, 0))[None]
-    at = [0, width, 2 * width, 3 * width, 3 * width + hidden]
-    o1 = at[4]
-    return (
-        y.reshape(1, seqs, slots, width),
-        gin.reshape(1, seqs, slots, width),
-        aw_g[None],
-        flat[:, o1 + 3 * width:],
-        ow_g[None],
-        flat[:, o1 + 2 * width:o1 + 3 * width],
-        flat[:, o1:o1 + width],
-        flat[:, o1 + width:o1 + 2 * width],
-        ew_g[None],
-        flat[:, 3 * width:o1],
-        rw_g[None],
-        flat[:, 2 * width:3 * width],
-        flat[:, :width],
-        flat[:, width:2 * width],
-    )
+        layer_input.reshape(total, width), cotangent.reshape(total, width), lengths, regions, weights, vectors)
+    grads = run_sums((act, gred, low, gexp, h, gproj, ctx, gatt), sums, lax.axis_size("dp"))
+    return (y.reshape(1, seqs, slots, width), gin.reshape(1, seqs, slots, width)) + tuple(
+        g[None] if g.shape[0] > 1 else g for g in grads)
 
 
 def solution(mesh):

time: 470 us -> 369 us (0.79)
  waiting for transfers between devices: 163 us -> 0 us
  Pallas kernels: 201 us -> 363 us
  blocking collectives: 30.9 us -> 0 us
  other arithmetic: 28 us -> 0 us
  matrix products: 23.8 us -> 0 us
  between operations: 14.1 us -> 0.68 us
    psum x1 -> x0, waiting for transfers between devices: 163 us -> none  [reduced(): return lax.psum(v.astype(bf16), 'dp').astype(f32)]
    pallas_call x0 -> x2, Pallas kernels: none -> 161 us  [the longest x1 142 us: run_sums(): pl.pallas_call(functools.partial(sum_kernel, dp), out_shape=(shape((units...]
    psum x1 -> x0, blocking collectives: 30.9 us -> none  [reduced(): return lax.psum(v.astype(bf16), 'dp').astype(f32)]
    dot_general x4 -> x0, matrix products: 23.8 us -> none  [tn(): lax.dot_general(left, right, (((0,), (0,)), ((), ())), preferred_element_...]
    broadcast_in_dim x5 -> x0, other arithmetic: 18.4 us -> none  [the longest x1 7.52 us: local(): ew_g[None]]
    convert_element_type x7 -> x0, other arithmetic: 8.9 us -> none  [local(): v.astype(f32)]
  transfers between devices with their start and end apart: 1 -> 0, of which waited for: 1 -> 0; matrix products, arithmetic and copies ran while one was open for 0% -> 0% of each run, Pallas kernels for 0% -> 0%
where the time goes in v2:
time: 369 us; the launch traced here: 368 us
  Pallas kernels  363 us (98%)
  local copies, waits for them, and re-layouts  4.12 us (1%)
    pallas_call x1, Pallas kernels, run_pipeline(): pl.pallas_call(functools.partial(pipeline_kernel, micro), out_shape=(shap...  202 us
    pallas_call x1, Pallas kernels, run_sums(): pl.pallas_call(functools.partial(sum_kernel, dp), out_shape=(shape((units...  142 us
    pallas_call x1, Pallas kernels, run_sums(): pl.pallas_call(functools.partial(write_kernel, hid_blocks, wide_blocks),...  18.6 us

profile of v2, /device:TPU:1, one launch (start us, length us, event | category | flops | bytes accessed | tf_op | source)
XLA Modules:
  0.0 368.1 jit_solution(5454891485201722501)
XLA Ops:
  0.7 202.4 %shard_map.263 = (bf16[1024,768]{1,0:T(8,128)(2,1)}, f32[1024,768]{1,0:T(8,128)}, bf16[1024,768]{1,0:T(8,128)(2,1)}, bf16[1024,768]{1,0:T(8,128)(2,1)}, bf16[102...) custom-call(bf16[1024,768]{1,0:T(8,128)(2,1)} %bitcast.21, ...), custom_call_target="tpu_custom_call" | custom-call | flops 28991029248 | bytes 40000000 | tf_op jit(solution)/shard_map/pallas_call | solution.py:363
  203.1 142.3 %shard_map.264 = (bf16[12,768,768]{2,1,0:T(8,128)(2,1)}, f32[8,1152]{1,0:T(8,128)}) custom-call(bf16[1024,3072]{1,0:T(8,128)(2,1)} %get-tuple-element.41.act_any, bf16[1024,768]{1,0:T(8,128)(2,1)} %get-tuple-element.42.gred_any, bf16[1024,768]{1,0:T(8,128)(2,1)} %get-tuple-element.43.low_any, bf16[1024,3072]{1,0:T(8,128)(2,1)} %get-tuple-element.44.gexp_any, ...), custom_call_target="tpu_custom_call" | custom-call | tf_op jit(solution)/shard_map/pallas_call | solution.py:637
  345.3 0.0 copy-start.1
  345.3 18.6 %shard_map.265 = (f32[768,2304]{1,0:T(8,128)}, f32[1,1536]{1,0:T(1,128)}, f32[768,768]{1,0:T(8,128)}, f32[1,768]{1,0:T(1,128)}, f32[1,768]{1,0:T(1,128)}, /*inde...) custom-call(bf16[12,768,768]{2,1,0:T(8,128)(2,1)} %get-tuple-element, ...), custom_call_target="tpu_custom_call" | custom-call | tf_op jit(solution)/shard_map/pallas_call | solution.py:668
  364.0 0.0 copy-start
  364.0 0.0 copy-done.1
  364.0 1.1 copy.32
  365.1 1.3 copy-done
  366.4 1.7 copy.33
Async XLA Ops:
  345.3 18.6 %copy-start.1 = (bf16[1024,768]{1,0:T(8,128)(2,1)S(1)}, bf16[1024,768]{1,0:T(8,128)(2,1)}, u32[]{:S(2)}) copy-start(bf16[1024,768]{1,0:T(8,128)(2,1)} %get-tuple-element.39) | copy-start | bytes 4718596
  364.0 2.5 copy-start

commit v3 on v2

--- a/solution.py
+++ b/solution.py
@@ -31,13 +31,8 @@
 
 
 def gelu_pair(x):
-    z = jnp.abs(x) * 0.7071067811865476
-    t = 1.0 / (1.0 + 0.3275911 * z)
-    e = jnp.exp(-0.5 * (x * x))
-    poly = t * (0.127414796 + t * (-0.142248368 + t * (0.7107068705 + t * (-0.7265760135 + t * 0.5307027145))))
-    tail = poly * e
-    phi = jnp.where(x >= 0, 1.0 - tail, tail)
-    return x * phi, phi + (x * 0.3989422804014327) * e
+    phi = 0.5 + 0.5 * lax.erf(x * 0.7071067811865476)
+    return x * phi, phi + (x * 0.3989422804014327) * jnp.exp2((x * x) * -0.7213475204444817)
 
 
 def fold(v):
@@ -49,7 +44,7 @@
     micro,
     x_any, ct_any, lengths, regions, aw, ow, ew, rw, ab_in, ob_in, g1_in, s1_in, eb_in, rb_in, g2_in, s2_in,
     y_out, gin_out, h_out, ctx_out, low_out, act_out, gred_out, gexp_out, gatt_out, gproj_out, sums,
-    ab, ob, g1, s1, eb, rb, g2, s2,
+    usable, gctx, ab, ob, g1, s1, eb, rb, g2, s2,
     h_ref, g_ref, y_ref, gb_ref, qkv, shares, gp, n1, r1, n2, r2,
     ctx, low, act, gred, gexp, gatt, gproj, gin, acc, mid,
     h_sem, g_sem, ysend_sem, yrecv_sem, gsend_sem, grecv_sem, y_sem, hs_sem,
@@ -123,6 +118,9 @@
     for dst, src in ((ob, ob_in), (g1, g1_in), (s1, s1_in), (eb, eb_in), (rb, rb_in), (g2, g2_in), (s2, s2_in)):
         dst[...] = src[...].astype(f32)
     position = lax.broadcasted_iota(jnp.int32, (1, slots), 1)
+    for seq in range(regions.shape[0]):
+        known = (position < lengths[seq]) | (regions[seq:seq + 1, :] == 1)
+        usable[seq] = jnp.broadcast_to(known.astype(f32), (8, slots))
     lane = lax.broadcasted_iota(jnp.int32, (slots, 128), 1)
     first_half = lane < 64
 
@@ -145,6 +143,18 @@
     staged_b = ((gred, gred_out, gred_sem), (gexp, gexp_out, gexp_sem), (gatt, gatt_out, gatt_sem),
                 (gproj, gproj_out, gproj_sem), (gin, gin_out, gin_sem))
 
+    combos = [(g, p) for p in range(pairs) for g in range(groups)]
+    blocks = [slice(b, b + BLOCK) for b in range(0, rows, BLOCK)]
+
+    def part_of(m, g, p, which):
+        at = which * width + p * 128
+        return qkv[m, g * slots:(g + 1) * slots, at:at + 128]
+
+    def stats():
+        means = [jnp.mean(acc[bs, :], -1, keepdims=True) for bs in blocks]
+        parts = [acc[bs, :] - mean for bs, mean in zip(blocks, means)]
+        return means, [lax.rsqrt(jnp.mean(c * c, -1, keepdims=True) + epsilon) for c in parts]
+
     def forward(m):
         slot = lax.rem(m, 2)
 
@@ -169,30 +179,24 @@
             if c < width:
                 p = p * 0.125
             qkv[m, :, c:c + 256] = p.astype(bf16)
-        for g in range(groups):
-            seq = m * groups + g
-            ok = (position < lengths[seq]) | (regions[pl.ds(seq, 1), :] == 1)
-            rs = slice(g * slots, (g + 1) * slots)
-            for p in range(pairs):
-                q = qkv[m, rs, p * 128:(p + 1) * 128]
-                k = qkv[m, rs, width + p * 128:width + (p + 1) * 128]
-                v = qkv[m, rs, 2 * width + p * 128:2 * width + (p + 1) * 128]
-                s = nt(stack(q), k)
-                s = jnp.where(ok, s, neg_large)
-                e = jnp.exp(s - jnp.max(s, -1, keepdims=True))
-                sh = (e * (1.0 / jnp.sum(e, -1, keepdims=True))).astype(bf16)
-                shares[m, g * pairs + p] = sh
-                ctx[slot, rs, p * 128:(p + 1) * 128] = unstack(nn(sh, v)).astype(bf16)
+        oks = [usable[m * groups + g, 0:1, :] > 0 for g in range(groups)]
+        ss = [jnp.where(oks[g], nt(stack(part_of(m, g, p, 0)), part_of(m, g, p, 1)), neg_large) for g, p in combos]
+        tops = [jnp.max(s, -1, keepdims=True) for s in ss]
+        es = [jnp.exp(s - top) for s, top in zip(ss, tops)]
+        invs = [1.0 / jnp.sum(e, -1, keepdims=True) for e in es]
+        for (g, p), e, inv in zip(combos, es, invs):
+            shares[m, g * pairs + p] = (e * inv).astype(bf16)
+        os = [nn(shares[m, g * pairs + p], part_of(m, g, p, 2)) for g, p in combos]
+        for (g, p), o in zip(combos, os):
+            ctx[slot, g * slots:(g + 1) * slots, p * 128:(p + 1) * 128] = unstack(o).astype(bf16)
         store(ctx, ctx_out, ctx_sem, m, slot).start()
         c_all = ctx[slot]
         for c in range(0, width, 256):
             acc[:, c:c + 256] = nn(c_all, ow[:, c:c + 256]) + ob[:, c:c + 256]
-        for b in range(0, rows, BLOCK):
-            bs = slice(b, b + BLOCK)
-            v = acc[bs, :] + h_ref[m, bs, :].astype(f32)
-            centre = v - jnp.mean(v, -1, keepdims=True)
-            inv = lax.rsqrt(jnp.mean(centre * centre, -1, keepdims=True) + epsilon)
-            normed = centre * inv
+        for bs in blocks:
+            acc[bs, :] += h_ref[m, bs, :].astype(f32)
+        for bs, mean, inv in zip(blocks, *stats()):
+            normed = (acc[bs, :] - mean) * inv
             out = normed * g1[...] + s1[...]
             n1[m, bs, :] = normed.astype(bf16)
             r1[m, bs, :] = jnp.broadcast_to(inv, (BLOCK, 128))
@@ -209,12 +213,10 @@
         a_all = act[slot]
         for c in range(0, width, 256):
             acc[:, c:c + 256] = nn(a_all, rw[:, c:c + 256]) + rb[:, c:c + 256]
-        for b in range(0, rows, BLOCK):
-            bs = slice(b, b + BLOCK)
-            v = acc[bs, :] + mid[bs, :]
-            centre = v - jnp.mean(v, -1, keepdims=True)
-            inv = lax.rsqrt(jnp.mean(centre * centre, -1, keepdims=True) + epsilon)
-            normed = centre * inv
+        for bs in blocks:
+            acc[bs, :] += mid[bs, :]
+        for bs, mean, inv in zip(blocks, *stats()):
+            normed = (acc[bs, :] - mean) * inv
             n2[m, bs, :] = normed.astype(bf16)
             r2[m, bs, :] = jnp.broadcast_to(inv, (BLOCK, 128))
             y_ref[m, bs, :] = (normed * g2[...] + s2[...]).astype(bf16)
@@ -225,10 +227,12 @@
 
         store(y_ref, y_out, y_sem, m, m).start()
 
-    def norm_back(grad, normed, inv, gain):
+    def norm_back(grad, normed, inv, gain, first, second):
+        return inv * (grad * gain - first - normed * second)
+
+    def norm_sums(grad, normed, gain):
         scaled = grad * gain
-        return inv * (scaled - jnp.mean(scaled, -1, keepdims=True)
-                      - normed * jnp.mean(scaled * normed, -1, keepdims=True))
+        return jnp.mean(scaled, -1, keepdims=True), jnp.mean(scaled * normed, -1, keepdims=True)
 
     def backward(m):
         slot = lax.rem(m, 2)
@@ -246,11 +250,11 @@
             for src, dst, sem in staged_b:
                 store(src, dst, sem, m - 2, slot).wait()
 
-        for b in range(0, rows, BLOCK):
-            bs = slice(b, b + BLOCK)
+        pairs_of = [norm_sums(g_ref[m, bs, :].astype(f32), n2[m, bs, :].astype(f32), g2[...]) for bs in blocks]
+        for bs, (one, two) in zip(blocks, pairs_of):
             go = g_ref[m, bs, :].astype(f32)
             normed = n2[m, bs, :].astype(f32)
-            mix = norm_back(go, normed, r2[m, bs, 0:1], g2[...])
+            mix = norm_back(go, normed, r2[m, bs, 0:1], g2[...], one, two)
             mid[bs, :] = mix
             gred[slot, bs, :] = mix.astype(bf16)
             sums[:, o_g2:o_g2 + width] += fold(go * normed)
@@ -266,11 +270,13 @@
         e_all = gexp[slot]
         for c in range(0, width, 256):
             acc[:, c:c + 256] = nt(e_all, ew[c:c + 256, :])
-        for b in range(0, rows, BLOCK):
-            bs = slice(b, b + BLOCK)
-            gf = acc[bs, :] + mid[bs, :]
+        for bs in blocks:
+            acc[bs, :] += mid[bs, :]
+        pairs_of = [norm_sums(acc[bs, :], n1[m, bs, :].astype(f32), g1[...]) for bs in blocks]
+        for bs, (one, two) in zip(blocks, pairs_of):
+            gf = acc[bs, :]
             normed = n1[m, bs, :].astype(f32)
-            gm = norm_back(gf, normed, r1[m, bs, 0:1], g1[...])
+            gm = norm_back(gf, normed, r1[m, bs, 0:1], g1[...], one, two)
             mid[bs, :] = gm
             gatt[slot, bs, :] = gm.astype(bf16)
             sums[:, o_g1:o_g1 + width] += fold(gf * normed)
@@ -279,27 +285,28 @@
         store(gatt, gatt_out, gatt_sem, m, slot).start()
         t_all = gatt[slot]
         for c in range(0, width, 256):
-            gc_all = nt(t_all, ow[c:c + 256, :]).astype(bf16)
-            for g in range(groups):
-                rs = slice(g * slots, (g + 1) * slots)
-                for half in range(2):
-                    p = c // 128 + half
-                    q = qkv[m, rs, p * 128:(p + 1) * 128]
-                    k = qkv[m, rs, width + p * 128:width + (p + 1) * 128]
-                    v = qkv[m, rs, 2 * width + p * 128:2 * width + (p + 1) * 128]
-                    shb = shares[m, g * pairs + p]
-                    sh = shb.astype(f32)
-                    gc2 = stack(gc_all[rs, half * 128:(half + 1) * 128])
-                    gs = nt(gc2, v)
-                    gv = tn(shb, gc2)
-                    gsc = (sh * (gs - jnp.sum(gs * sh, -1, keepdims=True))).astype(bf16)
-                    gq = unstack(nn(gsc, k)) * 0.125
-                    gk = tn(gsc, stack(q))
-                    gproj[slot, rs, p * 128:(p + 1) * 128] = gq.astype(bf16)
-                    gproj[slot, rs, width + p * 128:width + (p + 1) * 128] = gk.astype(bf16)
-                    gproj[slot, rs, 2 * width + p * 128:2 * width + (p + 1) * 128] = gv.astype(bf16)
-                    sums[:, o_q + p * 128:o_q + (p + 1) * 128] += fold(gq)
-                    sums[:, o_v + p * 128:o_v + (p + 1) * 128] += fold(gv)
+            gctx[:, c:c + 256] = nt(t_all, ow[c:c + 256, :]).astype(bf16)
+
+        def gc_of(g, p):
+            return stack(gctx[g * slots:(g + 1) * slots, p * 128:(p + 1) * 128])
+
+        def put(g, p, which, v):
+            at = which * width + p * 128
+            gproj[slot, g * slots:(g + 1) * slots, at:at + 128] = v.astype(bf16)
+
+        gss = [nt(gc_of(g, p), part_of(m, g, p, 2)) for g, p in combos]
+        gvs = [tn(shares[m, g * pairs + p], gc_of(g, p)) for g, p in combos]
+        dots = [jnp.sum(gs * shares[m, g * pairs + p].astype(f32), -1, keepdims=True) for (g, p), gs in zip(combos, gss)]
+        gscs = [(shares[m, g * pairs + p].astype(f32) * (gs - d)).astype(bf16)
+                for (g, p), gs, d in zip(combos, gss, dots)]
+        gqs = [unstack(nn(gsc, part_of(m, g, p, 1))) * 0.125 for (g, p), gsc in zip(combos, gscs)]
+        gks = [tn(gsc, stack(part_of(m, g, p, 0))) for (g, p), gsc in zip(combos, gscs)]
+        for (g, p), gq, gk, gv in zip(combos, gqs, gks, gvs):
+            put(g, p, 0, gq)
+            put(g, p, 1, gk)
+            put(g, p, 2, gv)
+            sums[:, o_q + p * 128:o_q + (p + 1) * 128] += fold(gq)
+            sums[:, o_v + p * 128:o_v + (p + 1) * 128] += fold(gv)
         store(gproj, gproj_out, gproj_sem, m, slot).start()
         p_all = gproj[slot]
         for c in range(0, width, 256):
@@ -313,12 +320,14 @@
 
         store(gin, gin_out, gin_sem, m, slot).start()
 
+    lag = jnp.where(stage == last, 0, micro - 1)
+
     def tick(i, carry):
         @pl.when(i < micro)
         def _():
             forward(i)
 
-        j = i - (last - stage)
+        j = i - lag
 
         @pl.when((j >= 0) & (j < micro))
         def _():
@@ -326,7 +335,7 @@
 
         return carry
 
-    lax.fori_loop(0, micro + last, tick, 0)
+    lax.fori_loop(0, 2 * micro - 1, tick, 0)
 
     for m in range(micro):
         store(h_ref, h_out, hs_sem, m, m).wait()
@@ -370,7 +379,7 @@
         ),
         in_specs=[hbm, hbm, pl.BlockSpec(memory_space=pltpu.SMEM)] + [vmem] * 13,
         out_specs=(hbm,) * 10 + (vmem,),
-        scratch_shapes=[pltpu.VMEM((1, n), f32) for n in (wide, width, width, width, hidden, width, width, width)] + [
+        scratch_shapes=[pltpu.VMEM((regions.shape[0], 8, slots), f32), pltpu.VMEM((rows, width), bf16)] + [pltpu.VMEM((1, n), f32) for n in (wide, width, width, width, hidden, width, width, width)] + [
             pltpu.VMEM((micro, rows, width), bf16),
             pltpu.VMEM((micro, rows, width), bf16),
             pltpu.VMEM((micro, rows, width), bf16),

time: 369 us -> 309 us (0.84)
  Pallas kernels: 363 us -> 304 us
    pallas_call x1, Pallas kernels: 202 us -> 145 us  [run_pipeline(): pl.pallas_call(functools.partial(pipeline_kernel, micro), out_shape=(shap...]
where the time goes in v3:
time: 309 us
  Pallas kernels  304 us (98%)
  local copies, waits for them, and re-layouts  4.12 us (1%)
    pallas_call x1, Pallas kernels, run_pipeline(): pl.pallas_call(functools.partial(pipeline_kernel, micro), out_shape=(shap...  145 us
    pallas_call x1, Pallas kernels, run_sums(): pl.pallas_call(functools.partial(sum_kernel, dp), out_shape=(shape((units...  140 us
    pallas_call x1, Pallas kernels, run_sums(): pl.pallas_call(functools.partial(write_kernel, hid_blocks, wide_blocks),...  18.6 us

profile of v3, /device:TPU:1, one launch (start us, length us, event | category | flops | bytes accessed | tf_op | source)
XLA Modules:
  0.0 308.6 jit_solution(7887611495475932812)
XLA Ops:
  0.7 144.7 %shard_map.263 = (bf16[1024,768]{1,0:T(8,128)(2,1)}, f32[1024,768]{1,0:T(8,128)}, bf16[1024,768]{1,0:T(8,128)(2,1)}, bf16[1024,768]{1,0:T(8,128)(2,1)}, bf16[102...) custom-call(bf16[1024,768]{1,0:T(8,128)(2,1)} %bitcast.21, ...), custom_call_target="tpu_custom_call" | custom-call | flops 28991029248 | bytes 40000000 | tf_op jit(solution)/shard_map/pallas_call | solution.py:372
  145.4 140.5 %shard_map.264 = (bf16[12,768,768]{2,1,0:T(8,128)(2,1)}, f32[8,1152]{1,0:T(8,128)}) custom-call(bf16[1024,3072]{1,0:T(8,128)(2,1)} %get-tuple-element.41.act_any, bf16[1024,768]{1,0:T(8,128)(2,1)} %get-tuple-element.42.gred_any, bf16[1024,768]{1,0:T(8,128)(2,1)} %get-tuple-element.43.low_any, bf16[1024,3072]{1,0:T(8,128)(2,1)} %get-tuple-element.44.gexp_any, ...), custom_call_target="tpu_custom_call" | custom-call | tf_op jit(solution)/shard_map/pallas_call | solution.py:646
  285.9 0.0 copy-start.1
  285.9 18.6 %shard_map.265 = (f32[768,2304]{1,0:T(8,128)}, f32[1,1536]{1,0:T(1,128)}, f32[768,768]{1,0:T(8,128)}, f32[1,768]{1,0:T(1,128)}, f32[1,768]{1,0:T(1,128)}, /*inde...) custom-call(bf16[12,768,768]{2,1,0:T(8,128)(2,1)} %get-tuple-element, ...), custom_call_target="tpu_custom_call" | custom-call | tf_op jit(solution)/shard_map/pallas_call | solution.py:677
  304.5 0.0 copy-start
  304.5 0.0 copy-done.1
  304.5 1.1 copy.32
  305.7 1.3 copy-done
  307.0 1.7 copy.33
Async XLA Ops:
  285.9 18.6 %copy-start.1 = (bf16[1024,768]{1,0:T(8,128)(2,1)S(1)}, bf16[1024,768]{1,0:T(8,128)(2,1)}, u32[]{:S(2)}) copy-start(bf16[1024,768]{1,0:T(8,128)(2,1)} %get-tuple-element.39) | copy-start | bytes 4718596
  304.5 2.5 copy-start

commit v4 on v3

--- a/solution.py
+++ b/solution.py
@@ -8,7 +8,7 @@
 from jax.sharding import PartitionSpec as P
 
 HEADS = 12
-GROUP = 2
+GROUP = 1
 BLOCK = 32
 CHUNK = 512
 epsilon = 1e-05
@@ -42,12 +42,12 @@
 
 def pipeline_kernel(
     micro,
-    x_any, ct_any, lengths, regions, aw, ow, ew, rw, ab_in, ob_in, g1_in, s1_in, eb_in, rb_in, g2_in, s2_in,
+    x_any, ct_any, lengths, regions, aw_any, ow_any, ew_any, rw_any, ab_in, ob_in, g1_in, s1_in, eb_in, rb_in, g2_in, s2_in,
     y_out, gin_out, h_out, ctx_out, low_out, act_out, gred_out, gexp_out, gatt_out, gproj_out, sums,
-    usable, gctx, ab, ob, g1, s1, eb, rb, g2, s2,
+    aw, ow, ew, rw, awt, owt, ewt, rwt, usable, gctx, ab, ob, g1, s1, eb, rb, g2, s2,
     h_ref, g_ref, y_ref, gb_ref, qkv, shares, gp, n1, r1, n2, r2,
     ctx, low, act, gred, gexp, gatt, gproj, gin, acc, mid,
-    h_sem, g_sem, ysend_sem, yrecv_sem, gsend_sem, grecv_sem, y_sem, hs_sem,
+    w_sem, h_sem, g_sem, ysend_sem, yrecv_sem, gsend_sem, grecv_sem, y_sem, hs_sem,
     ctx_sem, low_sem, act_sem, gred_sem, gexp_sem, gatt_sem, gproj_sem, gin_sem,
 ):
     stage = lax.axis_index("pipe")
@@ -81,11 +81,21 @@
     def store(src, dst, sem, m, slot):
         return pltpu.make_async_copy(src.at[slot], dst.at[pl.ds(m * rows, rows)], sem.at[slot])
 
+    filled = ((aw_any, aw), (ow_any, ow), (ew_any, ew), (rw_any, rw))
+
+    def load_w(k):
+        return pltpu.make_async_copy(filled[k][0], filled[k][1], w_sem.at[k])
+
+    load_w(0).start()
+
     @pl.when(stage == 0)
     def _():
         for m in range(micro):
             load_h(m).start()
 
+    for k in range(1, 4):
+        load_w(k).start()
+
     @pl.when(stage == last)
     def _():
         for m in range(micro):
@@ -101,6 +111,7 @@
     def _():
         pl.semaphore_signal(barrier, inc=1, device_id={"pipe": after}, device_id_type=MESH)
 
+    load_w(0).wait()
     inside = (stage > 0) & (stage < last)
 
     @pl.when(inside)
@@ -190,6 +201,12 @@
         for (g, p), o in zip(combos, os):
             ctx[slot, g * slots:(g + 1) * slots, p * 128:(p + 1) * 128] = unstack(o).astype(bf16)
         store(ctx, ctx_out, ctx_sem, m, slot).start()
+
+        @pl.when((m == 0) & (stage == 0))
+        def _():
+            for k in range(1, 4):
+                load_w(k).wait()
+
         c_all = ctx[slot]
         for c in range(0, width, 256):
             acc[:, c:c + 256] = nn(c_all, ow[:, c:c + 256]) + ob[:, c:c + 256]
@@ -263,13 +280,13 @@
         store(gred, gred_out, gred_sem, m, slot).start()
         r_all = gred[slot]
         for c in range(0, hidden, CHUNK):
-            ge = nt(r_all, rw[c:c + CHUNK, :]) * gp[m, :, c:c + CHUNK].astype(f32)
+            ge = nn(r_all, rwt[:, c:c + CHUNK]) * gp[m, :, c:c + CHUNK].astype(f32)
             gexp[slot, :, c:c + CHUNK] = ge.astype(bf16)
             sums[:, o_eb + c:o_eb + c + CHUNK] += fold(ge)
         store(gexp, gexp_out, gexp_sem, m, slot).start()
         e_all = gexp[slot]
         for c in range(0, width, 256):
-            acc[:, c:c + 256] = nt(e_all, ew[c:c + 256, :])
+            acc[:, c:c + 256] = nn(e_all, ewt[:, c:c + 256])
         for bs in blocks:
             acc[bs, :] += mid[bs, :]
         pairs_of = [norm_sums(acc[bs, :], n1[m, bs, :].astype(f32), g1[...]) for bs in blocks]
@@ -285,7 +302,7 @@
         store(gatt, gatt_out, gatt_sem, m, slot).start()
         t_all = gatt[slot]
         for c in range(0, width, 256):
-            gctx[:, c:c + 256] = nt(t_all, ow[c:c + 256, :]).astype(bf16)
+            gctx[:, c:c + 256] = nn(t_all, owt[:, c:c + 256]).astype(bf16)
 
         def gc_of(g, p):
             return stack(gctx[g * slots:(g + 1) * slots, p * 128:(p + 1) * 128])
@@ -310,7 +327,7 @@
         store(gproj, gproj_out, gproj_sem, m, slot).start()
         p_all = gproj[slot]
         for c in range(0, width, 256):
-            gi = nt(p_all, aw[c:c + 256, :]) + mid[:, c:c + 256]
+            gi = nn(p_all, awt[:, c:c + 256]) + mid[:, c:c + 256]
             gin[slot, :, c:c + 256] = gi
             gb_ref[m, :, c:c + 256] = gi.astype(bf16)
 
@@ -322,20 +339,38 @@
 
     lag = jnp.where(stage == last, 0, micro - 1)
 
-    def tick(i, carry):
-        @pl.when(i < micro)
-        def _():
-            forward(i)
-
-        j = i - lag
-
-        @pl.when((j >= 0) & (j < micro))
-        def _():
-            backward(j)
+    def turn():
+        @pl.when(stage > 0)
+        def _():
+            for k in range(1, 4):
+                load_w(k).wait()
+
+        one = (lax.broadcasted_iota(jnp.int32, (256, 256), 0) == lax.broadcasted_iota(jnp.int32, (256, 256), 1)).astype(f32).astype(bf16)
+        for src, dst in ((aw, awt), (ow, owt), (ew, ewt), (rw, rwt)):
+            def across(k, carry, src=src, dst=dst):
+                cols = pl.ds(pl.multiple_of(k * 256, 256), 256)
+                for r in range(0, dst.shape[0], 256):
+                    dst[r:r + 256, cols] = nt(one, src[cols, r:r + 256]).astype(bf16)
+                return carry
+
+            lax.fori_loop(0, src.shape[0] // 256, across, 0)
+
+    def tick(t, carry):
+        @pl.when((t >= 1) & (t <= micro))
+        def _():
+            forward(jnp.clip(t - 1, 0, micro - 1))
+
+        @pl.when(t == jnp.where(stage > 0, 0, lag + 1))
+        def _():
+            turn()
+
+        @pl.when((t >= lag + 1) & (t <= lag + micro))
+        def _():
+            backward(jnp.clip(t - 1 - lag, 0, micro - 1))
 
         return carry
 
-    lax.fori_loop(0, 2 * micro - 1, tick, 0)
+    lax.fori_loop(0, 2 * micro, tick, 0)
 
     for m in range(micro):
         store(h_ref, h_out, hs_sem, m, m).wait()
@@ -377,9 +412,9 @@
             shape((total, width), bf16), shape((total, hidden), bf16), shape((total, width), bf16),
             shape((total, wide), bf16), shape((8, sum_width), f32),
         ),
-        in_specs=[hbm, hbm, pl.BlockSpec(memory_space=pltpu.SMEM)] + [vmem] * 13,
+        in_specs=[hbm, hbm, pl.BlockSpec(memory_space=pltpu.SMEM), vmem] + [hbm] * 4 + [vmem] * 8,
         out_specs=(hbm,) * 10 + (vmem,),
-        scratch_shapes=[pltpu.VMEM((regions.shape[0], 8, slots), f32), pltpu.VMEM((rows, width), bf16)] + [pltpu.VMEM((1, n), f32) for n in (wide, width, width, width, hidden, width, width, width)] + [
+        scratch_shapes=[pltpu.VMEM(w.shape, bf16) for w in weights] + [pltpu.VMEM(w.shape[::-1], bf16) for w in weights] + [pltpu.VMEM((regions.shape[0], 8, slots), f32), pltpu.VMEM((rows, width), bf16)] + [pltpu.VMEM((1, n), f32) for n in (wide, width, width, width, hidden, width, width, width)] + [
             pltpu.VMEM((micro, rows, width), bf16),
             pltpu.VMEM((micro, rows, width), bf16),
             pltpu.VMEM((micro, rows, width), bf16),
@@ -401,7 +436,7 @@
             pltpu.VMEM((2, rows, width), f32),
             pltpu.VMEM((rows, width), f32),
             pltpu.VMEM((rows, width), f32),
-        ] + [dma((micro,))] * 8 + [dma((2,))] * 8,
+        ] + [dma((4,))] + [dma((micro,))] * 8 + [dma((2,))] * 8,
         compiler_params=pltpu.CompilerParams(
             collective_id=0, has_side_effects=True, vmem_limit_bytes=63 * 1024 * 1024),
         cost_estimate=pl.CostEstimate(flops=flops, bytes_accessed=40_000_000, transcendentals=total * hidden),

time: 309 us -> 286 us (0.926)
  Pallas kernels: 304 us -> 280 us
    pallas_call x1, Pallas kernels: 145 us -> 124 us  [run_pipeline(): pl.pallas_call(functools.partial(pipeline_kernel, micro), out_shape=(shap...]
where the time goes in v4:
time: 286 us; the launch traced here: 285 us
  Pallas kernels  280 us (98%)
  local copies, waits for them, and re-layouts  4.12 us (1%)
    pallas_call x1, Pallas kernels, run_sums(): pl.pallas_call(functools.partial(sum_kernel, dp), out_shape=(shape((units...  138 us
    pallas_call x1, Pallas kernels, run_pipeline(): pl.pallas_call(functools.partial(pipeline_kernel, micro), out_shape=(shap...  124 us
    pallas_call x1, Pallas kernels, run_sums(): pl.pallas_call(functools.partial(write_kernel, hid_blocks, wide_blocks),...  18.6 us

profile of v4, /device:TPU:1, one launch (start us, length us, event | category | flops | bytes accessed | tf_op | source)
XLA Modules:
  0.0 285.0 jit_solution(11758814959695807074)
XLA Ops:
  0.7 123.6 %shard_map.263 = (bf16[1024,768]{1,0:T(8,128)(2,1)}, f32[1024,768]{1,0:T(8,128)}, bf16[1024,768]{1,0:T(8,128)(2,1)}, bf16[1024,768]{1,0:T(8,128)(2,1)}, bf16[102...) custom-call(bf16[1024,768]{1,0:T(8,128)(2,1)} %bitcast.21, ...), custom_call_target="tpu_custom_call" | custom-call | flops 28991029248 | bytes 40000000 | tf_op jit(solution)/shard_map/pallas_call | solution.py:407
  124.3 137.9 %shard_map.264 = (bf16[12,768,768]{2,1,0:T(8,128)(2,1)}, f32[8,1152]{1,0:T(8,128)}) custom-call(bf16[1024,3072]{1,0:T(8,128)(2,1)} %get-tuple-element.41.act_any, bf16[1024,768]{1,0:T(8,128)(2,1)} %get-tuple-element.42.gred_any, bf16[1024,768]{1,0:T(8,128)(2,1)} %get-tuple-element.43.low_any, bf16[1024,3072]{1,0:T(8,128)(2,1)} %get-tuple-element.44.gexp_any, ...), custom_call_target="tpu_custom_call" | custom-call | tf_op jit(solution)/shard_map/pallas_call | solution.py:681
  262.2 0.0 copy-start.1
  262.2 18.6 %shard_map.265 = (f32[768,2304]{1,0:T(8,128)}, f32[1,1536]{1,0:T(1,128)}, f32[768,768]{1,0:T(8,128)}, f32[1,768]{1,0:T(1,128)}, f32[1,768]{1,0:T(1,128)}, /*inde...) custom-call(bf16[12,768,768]{2,1,0:T(8,128)(2,1)} %get-tuple-element, ...), custom_call_target="tpu_custom_call" | custom-call | tf_op jit(solution)/shard_map/pallas_call | solution.py:712
  280.8 0.0 copy-start
  280.8 0.0 copy-done.1
  280.8 1.1 copy.32
  282.0 1.3 copy-done
  283.3 1.7 copy.33
Async XLA Ops:
  262.2 18.6 %copy-start.1 = (bf16[1024,768]{1,0:T(8,128)(2,1)S(1)}, bf16[1024,768]{1,0:T(8,128)(2,1)}, u32[]{:S(2)}) copy-start(bf16[1024,768]{1,0:T(8,128)(2,1)} %get-tuple-element.39) | copy-start | bytes 4718596
  280.8 2.5 copy-start

commit v5 on v4

--- a/solution.py
+++ b/solution.py
@@ -11,6 +11,7 @@
 GROUP = 1
 BLOCK = 32
 CHUNK = 512
+PARTS = 4
 epsilon = 1e-05
 neg_large = -1000000000.0
 MESH = pl.DeviceIdType.MESH
@@ -451,7 +452,7 @@
     steps = dp.bit_length() - 1
     plane = steps - 1
     landed = rest[:steps]
-    left_sem, right_sem, send_sem, recv_sem, vsend_sem, vrecv_sem = rest[steps:]
+    left_sem, right_sem, send_sem, recv_sem, vsend_sem, vrecv_sem, out_sem = rest[steps:]
     units, rows, cols = part.shape
     me = lax.axis_index("dp")
     hid_blocks = act_any.shape[1] // cols
@@ -501,8 +502,9 @@
         peer = place(unit, step)[1]
         start, size = base(unit, step + 1)
         where = 2 * steps - 1 - step
+        own = part if step == steps - 1 else total
         return pltpu.make_async_remote_copy(
-            src_ref=total.at[unit, ds(start, size)], dst_ref=total.at[unit, ds(start, size)],
+            src_ref=own.at[unit, ds(start, size)], dst_ref=total.at[unit, ds(start, size)],
             send_sem=send_sem.at[where, unit], recv_sem=recv_sem.at[where, unit],
             device_id={"dp": peer}, device_id_type=MESH)
 
@@ -516,6 +518,11 @@
             src_ref=total.at[unit, there], dst_ref=total.at[unit, there],
             send_sem=send_sem.at[where, unit], recv_sem=recv_sem.at[where, unit],
             device_id={"dp": peer}, device_id_type=MESH)
+
+    def keep(unit):
+        start, size = base(unit, steps)
+        rs = ds(start, size)
+        return pltpu.make_async_copy(part.at[unit, rs], total.at[unit, rs], out_sem.at[unit])
 
     def vector_copy(step):
         peer = me + 2 ** step * (1 - 2 * bit_of(2 ** step))
@@ -549,10 +556,7 @@
             n = min(96, size - b)
             rs = ds(start + b, n)
             s = part[unit, rs, :].astype(f32) + landed[step][unit, b:b + n, :].astype(f32)
-            if step == steps - 1:
-                total[unit, rs, :] = s.astype(bf16)
-            else:
-                part[unit, rs, :] = s.astype(bf16)
+            part[unit, rs, :] = s.astype(bf16)
 
     def when_unit(unit, body):
         @pl.when((unit >= 0) & (unit < units))
@@ -583,11 +587,14 @@
                 reduce_copy(unit, step + 1).start()
             else:
                 gather_copy(unit, step).start()
+                keep(unit).start()
         return body
 
     def gather_next(step):
         def body(unit):
             gather_arrival(unit, step).wait_recv()
+            if step == steps - 1:
+                keep(unit).wait()
             if step > 0:
                 gather_copy(unit, step - 1).start()
         return body
@@ -630,39 +637,58 @@
         vector_copy(step).wait_send()
 
 
-def write_kernel(hid_blocks, wide_blocks, total, vector, aw_g, ab_g, ow_g, ob_g, g1_g, s1_g, ew_g, eb_g, rw_g, rb_g, g2_g, s2_g):
-    t = pl.program_id(0)
-    first, second = hid_blocks, 2 * hid_blocks
-    third = second + wide_blocks
-
-    @pl.when(t == 0)
-    def _():
-        piece = vector.shape[1] // 3
-        at = 0
-        for out in (g2_g, s2_g, rb_g, eb_g, g1_g, s1_g, ob_g, ab_g):
-            for k in range(out.shape[1] // piece):
-                r, c = at // 3, at % 3
-                out[:, k * piece:(k + 1) * piece] = vector[r:r + 1, c * piece:(c + 1) * piece]
-                at += 1
-
-    @pl.when(t < first)
-    def _():
-        rw_g[...] = total[...].astype(f32)
-
-    @pl.when((t >= first) & (t < second))
-    def _():
-        ew_g[...] = total[...].astype(f32)
-
-    @pl.when((t >= second) & (t < third))
-    def _():
-        aw_g[...] = total[...].astype(f32)
-
-    @pl.when(t >= third)
-    def _():
-        ow_g[...] = total[...].astype(f32)
-
-
-def run_sums(parts, sums, dp):
+def write_kernel(hid_blocks, wide_blocks, total, vector, y, gin, y_g, gin_g, aw_g, ab_g, ow_g, ob_g, g1_g, s1_g, ew_g, eb_g, rw_g, rb_g, g2_g, s2_g, taken, given, y_buf, gin_buf, move_sem, in_sem, out_sem):
+    depth, rows, cols = taken.shape
+    places = (
+        [(rw_g, k, 0) for k in range(hid_blocks)] + [(ew_g, 0, k) for k in range(hid_blocks)]
+        + [(aw_g, 0, k) for k in range(wide_blocks)] + [(ow_g, 0, 0)]
+    )
+    split, span = cols // rows, total.shape[1] // cols
+    chunks = [(block, part) for block in range(len(places)) for part in range(split)]
+
+    def bring(k):
+        block, part = chunks[k]
+        start = (block % span) * cols + part * rows
+        return pltpu.make_async_copy(total.at[block // span, pl.ds(start, rows)], taken.at[k % depth], in_sem.at[k % depth])
+
+    def give(k):
+        block, part = chunks[k]
+        out, i, j = places[block]
+        target = out.at[pl.ds(i * cols + part * rows, rows), pl.ds(j * cols, cols)]
+        return pltpu.make_async_copy(given.at[k % depth], target, out_sem.at[k % depth])
+
+    ins = (pltpu.make_async_copy(y, y_buf, move_sem.at[0]), pltpu.make_async_copy(gin, gin_buf, move_sem.at[1]))
+    outs = (pltpu.make_async_copy(y_buf, y_g, move_sem.at[2]), pltpu.make_async_copy(gin_buf, gin_g, move_sem.at[3]))
+    for k in range(depth):
+        bring(k).start()
+    for move in ins:
+        move.start()
+    piece = vector.shape[1] // 3
+    at = 0
+    for out in (g2_g, s2_g, rb_g, eb_g, g1_g, s1_g, ob_g, ab_g):
+        for k in range(out.shape[1] // piece):
+            r, c = at // 3, at % 3
+            out[:, k * piece:(k + 1) * piece] = vector[r:r + 1, c * piece:(c + 1) * piece]
+            at += 1
+    for k in range(len(chunks)):
+        bring(k).wait()
+        if k >= depth:
+            give(k - depth).wait()
+        given[k % depth] = taken[k % depth].astype(f32)
+        give(k).start()
+        if k + depth < len(chunks):
+            bring(k + depth).start()
+        if k == depth:
+            for arrived, move in zip(ins, outs):
+                arrived.wait()
+                move.start()
+    for k in range(len(chunks) - depth, len(chunks)):
+        give(k).wait()
+    for move in outs:
+        move.wait()
+
+
+def run_sums(parts, sums, y, gin, dp):
     act, gred, low, gexp, h, gproj, ctx, gatt = parts
     total_rows, width = h.shape
     hidden, wide = act.shape[1], gproj.shape[1]
@@ -682,41 +708,45 @@
         functools.partial(sum_kernel, dp),
         out_shape=(shape((units, unit_rows, width), bf16), shape((8, lanes), f32)),
         in_specs=[hbm] * 8 + [vmem],
-        out_specs=(vmem, vmem),
+        out_specs=(hbm, vmem),
         scratch_shapes=[
             pltpu.VMEM((units, unit_rows, width), bf16),
             pltpu.VMEM((2, total_rows, width), bf16),
             pltpu.VMEM((2, total_rows, width), bf16),
             pltpu.VMEM((2 * steps, 8, lanes), f32),
         ] + [pltpu.VMEM((units, unit_rows // 2 ** (k + 1), width), bf16) for k in range(steps)] + [
-            dma((2,)), dma((2,)), dma((2 * steps, units)), dma((2 * steps, units)), dma((steps,)), dma((steps,)),
+            dma((2,)), dma((2,)), dma((2 * steps, units)), dma((2 * steps, units)), dma((steps,)), dma((steps,)), dma((units,)),
         ],
         compiler_params=pltpu.CompilerParams(
-            collective_id=1, has_side_effects=True, vmem_limit_bytes=63 * 1024 * 1024),
+            collective_id=1, has_side_effects=True, vmem_limit_bytes=58 * 1024 * 1024),
     )(act, gred, low, gexp, h, gproj, ctx, gatt, sums)
 
     def one(count):
-        return shape((1, count), f32), pl.BlockSpec((1, count), lambda t: (0, 0))
-
-    a, b = hid_blocks, 2 * hid_blocks
+        return shape((1, count), f32), vmem
+
     outs = [
-        (shape((width, wide), f32), pl.BlockSpec((width, width), lambda t: (0, jnp.clip(t - b, 0, wide_blocks - 1)))),
+        (shape(y.shape, y.dtype), hbm), (shape(gin.shape, gin.dtype), hbm),
+        (shape((width, wide), f32), hbm),
         one(2 * width),
-        (shape((width, width), f32), pl.BlockSpec((width, width), lambda t: (0, 0))),
+        (shape((width, width), f32), hbm),
         one(width), one(width), one(width),
-        (shape((width, hidden), f32), pl.BlockSpec((width, width), lambda t: (0, jnp.clip(t - a, 0, hid_blocks - 1)))),
+        (shape((width, hidden), f32), hbm),
         one(hidden),
-        (shape((hidden, width), f32), pl.BlockSpec((width, width), lambda t: (jnp.clip(t, 0, hid_blocks - 1), 0))),
+        (shape((hidden, width), f32), hbm),
         one(width), one(width), one(width),
     ]
     return pl.pallas_call(
         functools.partial(write_kernel, hid_blocks, wide_blocks),
-        grid=(blocks,),
         out_shape=tuple(o[0] for o in outs),
-        in_specs=[pl.BlockSpec((None, width, width), lambda t: (t, 0, 0)), pl.BlockSpec((8, lanes), lambda t: (0, 0))],
+        in_specs=[hbm, vmem, hbm, hbm],
         out_specs=tuple(o[1] for o in outs),
-        compiler_params=pltpu.CompilerParams(vmem_limit_bytes=60 * 1024 * 1024),
-    )(total.reshape(blocks, width, width), vector)
+        scratch_shapes=[
+            pltpu.VMEM((PARTS, width // 2, width), bf16), pltpu.VMEM((PARTS, width // 2, width), f32),
+            pltpu.VMEM(y.shape, y.dtype), pltpu.VMEM(gin.shape, gin.dtype),
+            dma((4,)), dma((PARTS,)), dma((PARTS,)),
+        ],
+        compiler_params=pltpu.CompilerParams(vmem_limit_bytes=52 * 1024 * 1024),
+    )(total, vector, y, gin)
 
 
 def local(
@@ -730,7 +760,7 @@
     weights = (attend_weight[0], output_weight[0], expand_weight[0], reduce_weight[0])
     y, gin, h, ctx, low, act, gred, gexp, gatt, gproj, sums = run_pipeline(
         layer_input.reshape(total, width), cotangent.reshape(total, width), lengths, regions, weights, vectors)
-    grads = run_sums((act, gred, low, gexp, h, gproj, ctx, gatt), sums, lax.axis_size("dp"))
+    y, gin, *grads = run_sums((act, gred, low, gexp, h, gproj, ctx, gatt), sums, y, gin, lax.axis_size("dp"))
     return (y.reshape(1, seqs, slots, width), gin.reshape(1, seqs, slots, width)) + tuple(
         g[None] if g.shape[0] > 1 else g for g in grads)
 

time: 286 us -> 277 us (0.969)
  Pallas kernels: 280 us -> 275 us
  local copies, waits for them, and re-layouts: 4.12 us -> 0.77 us
    pallas_call x1, Pallas kernels: 138 us -> 134 us  [run_sums(): pl.pallas_call(functools.partial(sum_kernel, dp), out_shape=(shape((units...]
    unnamed x6 -> x4, local copies, waits for them, and re-layouts: 4.12 us -> 0.77 us
where the time goes in v5:
time: 277 us
  Pallas kernels  275 us (99%)
    pallas_call x1, Pallas kernels, run_sums(): pl.pallas_call(functools.partial(sum_kernel, dp), out_shape=(shape((units...  134 us
    pallas_call x1, Pallas kernels, run_pipeline(): pl.pallas_call(functools.partial(pipeline_kernel, micro), out_shape=(shap...  124 us
    pallas_call x1, Pallas kernels, run_sums(): pl.pallas_call(functools.partial(write_kernel, hid_blocks, wide_blocks),...  17.4 us

profile of v5, /device:TPU:1, one launch (start us, length us, event | category | flops | bytes accessed | tf_op | source)
XLA Modules:
  0.0 276.8 jit_solution(2737830017335837203)
XLA Ops:
  0.7 123.6 %shard_map.263 = (bf16[1024,768]{1,0:T(8,128)(2,1)}, f32[1024,768]{1,0:T(8,128)}, bf16[1024,768]{1,0:T(8,128)(2,1)}, bf16[1024,768]{1,0:T(8,128)(2,1)}, bf16[102...) custom-call(bf16[1024,768]{1,0:T(8,128)(2,1)} %bitcast.20, ...), custom_call_target="tpu_custom_call" | custom-call | flops 28991029248 | bytes 40000000 | tf_op jit(solution)/shard_map/pallas_call | solution.py:408
  124.3 0.0 copy-start
  124.3 134.3 %shard_map.264 = (bf16[12,768,768]{2,1,0:T(8,128)(2,1)}, f32[8,1152]{1,0:T(8,128)}) custom-call(bf16[1024,3072]{1,0:T(8,128)(2,1)} %get-tuple-element.41.act_any, bf16[1024,768]{1,0:T(8,128)(2,1)} %get-tuple-element.42.gred_any, bf16[1024,768]{1,0:T(8,128)(2,1)} %get-tuple-element.43.low_any, bf16[1024,3072]{1,0:T(8,128)(2,1)} %get-tuple-element.44.gexp_any, ...), custom_call_target="tpu_custom_call" | custom-call | tf_op jit(solution)/shard_map/pallas_call | solution.py:707
  258.6 0.0 copy-done
  258.6 0.0 copy-start.1
  258.6 0.8 copy-done.1
  259.4 17.4 %shard_map.265 = (bf16[1024,768]{1,0:T(8,128)(2,1)}, f32[1024,768]{1,0:T(8,128)}, f32[768,2304]{1,0:T(8,128)}, f32[1,1536]{1,0:T(1,128)}, f32[768,768]{1,0:T(8,1...) custom-call(bf16[12,768,768]{2,1,0:T(8,128)(2,1)} %get-tuple-element, ...), custom_call_target="tpu_custom_call" | custom-call | tf_op jit(solution)/shard_map/pallas_call | solution.py:738
Async XLA Ops:
  124.3 134.3 %copy-start = (bf16[1024,768]{1,0:T(8,128)(2,1)S(1)}, bf16[1024,768]{1,0:T(8,128)(2,1)}, u32[]{:S(2)}) copy-start(bf16[1024,768]{1,0:T(8,128)(2,1)} %get-tuple-element.52.y) | copy-start | bytes 4718596
  258.6 0.8 copy-start.1

commit v6 on v5

--- a/solution.py
+++ b/solution.py
@@ -45,7 +45,7 @@
     micro,
     x_any, ct_any, lengths, regions, aw_any, ow_any, ew_any, rw_any, ab_in, ob_in, g1_in, s1_in, eb_in, rb_in, g2_in, s2_in,
     y_out, gin_out, h_out, ctx_out, low_out, act_out, gred_out, gexp_out, gatt_out, gproj_out, sums,
-    aw, ow, ew, rw, awt, owt, ewt, rwt, usable, gctx, ab, ob, g1, s1, eb, rb, g2, s2,
+    aw, ow, ew, rw, awt, owt, ewt, rwt, usable, gctx, fresh, ab, ob, g1, s1, eb, rb, g2, s2,
     h_ref, g_ref, y_ref, gb_ref, qkv, shares, gp, n1, r1, n2, r2,
     ctx, low, act, gred, gexp, gatt, gproj, gin, acc, mid,
     w_sem, h_sem, g_sem, ysend_sem, yrecv_sem, gsend_sem, grecv_sem, y_sem, hs_sem,
@@ -221,18 +221,25 @@
             mid[bs, :] = out
             low[slot, bs, :] = out.astype(bf16)
         store(low, low_out, low_sem, m, slot).start()
-        l_all = low[slot]
+        def widen(c):
+            fresh[c // CHUNK % 2] = nn(low[slot], ew[:, c:c + CHUNK])
+
+        def narrow(c):
+            acc[...] += nn(act[slot, :, c:c + CHUNK], rw[c:c + CHUNK, :])
+
+        widen(0)
         for c in range(0, hidden, CHUNK):
-            x = nn(l_all, ew[:, c:c + CHUNK]) + eb[:, c:c + CHUNK]
-            a, d = gelu_pair(x)
+            if c + CHUNK < hidden:
+                widen(c + CHUNK)
+            if c > 0:
+                narrow(c - CHUNK)
+            else:
+                acc[...] = mid[...] + rb[...]
+            a, d = gelu_pair(fresh[c // CHUNK % 2] + eb[:, c:c + CHUNK])
             act[slot, :, c:c + CHUNK] = a.astype(bf16)
             gp[m, :, c:c + CHUNK] = d.astype(bf16)
         store(act, act_out, act_sem, m, slot).start()
-        a_all = act[slot]
-        for c in range(0, width, 256):
-            acc[:, c:c + 256] = nn(a_all, rw[:, c:c + 256]) + rb[:, c:c + 256]
-        for bs in blocks:
-            acc[bs, :] += mid[bs, :]
+        narrow(hidden - CHUNK)
         for bs, mean, inv in zip(blocks, *stats()):
             normed = (acc[bs, :] - mean) * inv
             n2[m, bs, :] = normed.astype(bf16)
@@ -415,7 +422,7 @@
         ),
         in_specs=[hbm, hbm, pl.BlockSpec(memory_space=pltpu.SMEM), vmem] + [hbm] * 4 + [vmem] * 8,
         out_specs=(hbm,) * 10 + (vmem,),
-        scratch_shapes=[pltpu.VMEM(w.shape, bf16) for w in weights] + [pltpu.VMEM(w.shape[::-1], bf16) for w in weights] + [pltpu.VMEM((regions.shape[0], 8, slots), f32), pltpu.VMEM((rows, width), bf16)] + [pltpu.VMEM((1, n), f32) for n in (wide, width, width, width, hidden, width, width, width)] + [
+        scratch_shapes=[pltpu.VMEM(w.shape, bf16) for w in weights] + [pltpu.VMEM(w.shape[::-1], bf16) for w in weights] + [pltpu.VMEM((regions.shape[0], 8, slots), f32), pltpu.VMEM((rows, width), bf16), pltpu.VMEM((2, rows, CHUNK), f32)] + [pltpu.VMEM((1, n), f32) for n in (wide, width, width, width, hidden, width, width, width)] + [
             pltpu.VMEM((micro, rows, width), bf16),
             pltpu.VMEM((micro, rows, width), bf16),
             pltpu.VMEM((micro, rows, width), bf16),
@@ -637,7 +644,7 @@
         vector_copy(step).wait_send()
 
 
-def write_kernel(hid_blocks, wide_blocks, total, vector, y, gin, y_g, gin_g, aw_g, ab_g, ow_g, ob_g, g1_g, s1_g, ew_g, eb_g, rw_g, rb_g, g2_g, s2_g, taken, given, y_buf, gin_buf, move_sem, in_sem, out_sem):
+def write_kernel(hid_blocks, wide_blocks, total, vector_any, y, gin, y_g, gin_g, aw_g, ab_g, ow_g, ob_g, g1_g, s1_g, ew_g, eb_g, rw_g, rb_g, g2_g, s2_g, taken, given, y_buf, gin_buf, vector, move_sem, in_sem, out_sem):
     depth, rows, cols = taken.shape
     places = (
         [(rw_g, k, 0) for k in range(hid_blocks)] + [(ew_g, 0, k) for k in range(hid_blocks)]
@@ -659,10 +666,13 @@
 
     ins = (pltpu.make_async_copy(y, y_buf, move_sem.at[0]), pltpu.make_async_copy(gin, gin_buf, move_sem.at[1]))
     outs = (pltpu.make_async_copy(y_buf, y_g, move_sem.at[2]), pltpu.make_async_copy(gin_buf, gin_g, move_sem.at[3]))
+    vector_copy = pltpu.make_async_copy(vector_any, vector, move_sem.at[4])
+    vector_copy.start()
     for k in range(depth):
         bring(k).start()
     for move in ins:
         move.start()
+    vector_copy.wait()
     piece = vector.shape[1] // 3
     at = 0
     for out in (g2_g, s2_g, rb_g, eb_g, g1_g, s1_g, ob_g, ab_g):
@@ -738,12 +748,12 @@
     return pl.pallas_call(
         functools.partial(write_kernel, hid_blocks, wide_blocks),
         out_shape=tuple(o[0] for o in outs),
-        in_specs=[hbm, vmem, hbm, hbm],
+        in_specs=[hbm] * 4,
         out_specs=tuple(o[1] for o in outs),
         scratch_shapes=[
             pltpu.VMEM((PARTS, width // 2, width), bf16), pltpu.VMEM((PARTS, width // 2, width), f32),
             pltpu.VMEM(y.shape, y.dtype), pltpu.VMEM(gin.shape, gin.dtype),
-            dma((4,)), dma((PARTS,)), dma((PARTS,)),
+            pltpu.VMEM((8, lanes), f32), dma((5,)), dma((PARTS,)), dma((PARTS,)),
         ],
         compiler_params=pltpu.CompilerParams(vmem_limit_bytes=52 * 1024 * 1024),
     )(total, vector, y, gin)

time: 277 us -> 274 us (0.989)
  Pallas kernels: 275 us -> 272 us
    pallas_call x1, Pallas kernels: 124 us -> 120 us  [run_pipeline(): pl.pallas_call(functools.partial(pipeline_kernel, micro), out_shape=(shap...]
where the time goes in v6:
time: 274 us; the launch traced here: 273 us
  Pallas kernels  272 us (99%)
    pallas_call x1, Pallas kernels, run_sums(): pl.pallas_call(functools.partial(sum_kernel, dp), out_shape=(shape((units...  134 us
    pallas_call x1, Pallas kernels, run_pipeline(): pl.pallas_call(functools.partial(pipeline_kernel, micro), out_shape=(shap...  120 us
    pallas_call x1, Pallas kernels, run_sums(): pl.pallas_call(functools.partial(write_kernel, hid_blocks, wide_blocks),...  17.5 us

profile of v6, /device:TPU:1, one launch (start us, length us, event | category | flops | bytes accessed | tf_op | source)
XLA Modules:
  0.0 273.4 jit_solution(13529399512527632610)
XLA Ops:
  0.7 120.2 %shard_map.263 = (bf16[1024,768]{1,0:T(8,128)(2,1)}, f32[1024,768]{1,0:T(8,128)}, bf16[1024,768]{1,0:T(8,128)(2,1)}, bf16[1024,768]{1,0:T(8,128)(2,1)}, bf16[102...) custom-call(bf16[1024,768]{1,0:T(8,128)(2,1)} %bitcast.20, ...), custom_call_target="tpu_custom_call" | custom-call | flops 28991029248 | bytes 40000000 | tf_op jit(solution)/shard_map/pallas_call | solution.py:415
  120.8 0.0 copy-start
  120.8 134.3 %shard_map.264 = (bf16[12,768,768]{2,1,0:T(8,128)(2,1)}, f32[8,1152]{1,0:T(8,128)}) custom-call(bf16[1024,3072]{1,0:T(8,128)(2,1)} %get-tuple-element.41.act_any, bf16[1024,768]{1,0:T(8,128)(2,1)} %get-tuple-element.42.gred_any, bf16[1024,768]{1,0:T(8,128)(2,1)} %get-tuple-element.43.low_any, bf16[1024,3072]{1,0:T(8,128)(2,1)} %get-tuple-element.44.gexp_any, ...), custom_call_target="tpu_custom_call" | custom-call | tf_op jit(solution)/shard_map/pallas_call | solution.py:717
  255.1 0.0 copy-done
  255.1 0.0 copy-start.1
  255.1 0.8 copy-done.1
  255.9 17.5 %shard_map.265 = (bf16[1024,768]{1,0:T(8,128)(2,1)}, f32[1024,768]{1,0:T(8,128)}, f32[768,2304]{1,0:T(8,128)}, f32[1,1536]{1,0:T(1,128)}, f32[768,768]{1,0:T(8,1...) custom-call(bf16[12,768,768]{2,1,0:T(8,128)(2,1)} %get-tuple-element, ...), custom_call_target="tpu_custom_call" | custom-call | tf_op jit(solution)/shard_map/pallas_call | solution.py:748
Async XLA Ops:
  120.8 134.3 %copy-start = (bf16[1024,768]{1,0:T(8,128)(2,1)S(1)}, bf16[1024,768]{1,0:T(8,128)(2,1)}, u32[]{:S(2)}) copy-start(bf16[1024,768]{1,0:T(8,128)(2,1)} %get-tuple-element.52.y) | copy-start | bytes 4718596
  255.1 0.8 copy-start.1

commit v7 on v6

--- a/solution.py
+++ b/solution.py
@@ -286,17 +286,25 @@
             sums[:, o_s2:o_s2 + width] += fold(go)
             sums[:, o_rb:o_rb + width] += fold(mix)
         store(gred, gred_out, gred_sem, m, slot).start()
-        r_all = gred[slot]
+        def widen(c):
+            fresh[c // CHUNK % 2] = nn(gred[slot], rwt[:, c:c + CHUNK])
+
+        def narrow(c):
+            acc[...] += nn(gexp[slot, :, c:c + CHUNK], ewt[c:c + CHUNK, :])
+
+        widen(0)
         for c in range(0, hidden, CHUNK):
-            ge = nn(r_all, rwt[:, c:c + CHUNK]) * gp[m, :, c:c + CHUNK].astype(f32)
+            if c + CHUNK < hidden:
+                widen(c + CHUNK)
+            if c > 0:
+                narrow(c - CHUNK)
+            else:
+                acc[...] = mid[...]
+            ge = fresh[c // CHUNK % 2] * gp[m, :, c:c + CHUNK].astype(f32)
             gexp[slot, :, c:c + CHUNK] = ge.astype(bf16)
             sums[:, o_eb + c:o_eb + c + CHUNK] += fold(ge)
         store(gexp, gexp_out, gexp_sem, m, slot).start()
-        e_all = gexp[slot]
-        for c in range(0, width, 256):
-            acc[:, c:c + 256] = nn(e_all, ewt[:, c:c + 256])
-        for bs in blocks:
-            acc[bs, :] += mid[bs, :]
+        narrow(hidden - CHUNK)
         pairs_of = [norm_sums(acc[bs, :], n1[m, bs, :].astype(f32), g1[...]) for bs in blocks]
         for bs, (one, two) in zip(blocks, pairs_of):
             gf = acc[bs, :]

time: 274 us -> 272 us (level)
  no operation moved by 1% of the time
where the time goes in v7:
time: 272 us
  Pallas kernels  271 us (100%)
    pallas_call x1, Pallas kernels, run_sums(): pl.pallas_call(functools.partial(sum_kernel, dp), out_shape=(shape((units...  134 us
    pallas_call x1, Pallas kernels, run_pipeline(): pl.pallas_call(functools.partial(pipeline_kernel, micro), out_shape=(shap...  119 us
    pallas_call x1, Pallas kernels, run_sums(): pl.pallas_call(functools.partial(write_kernel, hid_blocks, wide_blocks),...  17.5 us

profile of v7, /device:TPU:1, one launch (start us, length us, event | category | flops | bytes accessed | tf_op | source)
XLA Modules:
  0.0 272.0 jit_solution(13703921050326183303)
XLA Ops:
  0.7 118.9 %shard_map.263 = (bf16[1024,768]{1,0:T(8,128)(2,1)}, f32[1024,768]{1,0:T(8,128)}, bf16[1024,768]{1,0:T(8,128)(2,1)}, bf16[1024,768]{1,0:T(8,128)(2,1)}, bf16[102...) custom-call(bf16[1024,768]{1,0:T(8,128)(2,1)} %bitcast.20, ...), custom_call_target="tpu_custom_call" | custom-call | flops 28991029248 | bytes 40000000 | tf_op jit(solution)/shard_map/pallas_call | solution.py:423
  119.5 0.0 copy-start
  119.5 134.2 %shard_map.264 = (bf16[12,768,768]{2,1,0:T(8,128)(2,1)}, f32[8,1152]{1,0:T(8,128)}) custom-call(bf16[1024,3072]{1,0:T(8,128)(2,1)} %get-tuple-element.41.act_any, bf16[1024,768]{1,0:T(8,128)(2,1)} %get-tuple-element.42.gred_any, bf16[1024,768]{1,0:T(8,128)(2,1)} %get-tuple-element.43.low_any, bf16[1024,3072]{1,0:T(8,128)(2,1)} %get-tuple-element.44.gexp_any, ...), custom_call_target="tpu_custom_call" | custom-call | tf_op jit(solution)/shard_map/pallas_call | solution.py:725
  253.7 0.0 copy-done
  253.7 0.0 copy-start.1
  253.7 0.8 copy-done.1
  254.5 17.5 %shard_map.265 = (bf16[1024,768]{1,0:T(8,128)(2,1)}, f32[1024,768]{1,0:T(8,128)}, f32[768,2304]{1,0:T(8,128)}, f32[1,1536]{1,0:T(1,128)}, f32[768,768]{1,0:T(8,1...) custom-call(bf16[12,768,768]{2,1,0:T(8,128)(2,1)} %get-tuple-element, ...), custom_call_target="tpu_custom_call" | custom-call | tf_op jit(solution)/shard_map/pallas_call | solution.py:756
Async XLA Ops:
  119.5 134.2 %copy-start = (bf16[1024,768]{1,0:T(8,128)(2,1)S(1)}, bf16[1024,768]{1,0:T(8,128)(2,1)}, u32[]{:S(2)}) copy-start(bf16[1024,768]{1,0:T(8,128)(2,1)} %get-tuple-element.52.y) | copy-start | bytes 4718596
  253.7 0.8 copy-start.1
